TPU v7x, 512 devices: a whole 4x4x16 slice. The times are simulated.
512 devices in a mesh: dp: 16 (over x, z_hi, core), tm: 8 (over z_lo), height: 4 (over y).
Axes of the slice: x: 4, y: 4, z: 16 (z_hi: 2, z_lo: 8; z = z_hi * 8 + z_lo), core: 2. Of those that a mesh axis runs over, the one named last changes fastest.
Arguments:
- latent: bfloat16 [256, 8, 16, 512], P(('dp', 'tm'), None, None, 'height'), parts along dimension 0, may hold values from -6 to 6
- gain_latent: float32 [512], P('height'), may hold values from 0.25 to 1.75
- shift_latent: float32 [512], P('height'), may hold values from -3 to 3
- conv_latent: bfloat16 [13824, 512], P('tm', 'height'), may hold values from -0.0546875 to 0.0546875
- up_weight: bfloat16 [512, 2048], P('height'), may hold values from -0.25 to 0.25
- gain_block: float32 [256], replicated, may hold values from 0.25 to 1.75
- shift_block: float32 [256], replicated, may hold values from -3 to 3
- conv_block: bfloat16 [6912, 256], P(('tm', 'height')), may hold values from -0.078125 to 0.078125
- cotangent: bfloat16 [512, 16, 32, 256], P(('dp', 'tm'), 'height'), parts along dimension 0, may hold values from -6 to 6
Outputs:
- decoded: bfloat16 [512, 16, 32, 256], P(('dp', 'tm'), 'height'), parts along dimension 0
- grad_upsampled: bfloat16 [512, 16, 32, 256], P(('dp', 'tm'), 'height'), parts along dimension 0
- grad_weight: float32 [36864, 256], P(('dp', 'tm', 'height')), parts along dimension 0
- grad_gain: float32 [4096], P('dp'), parts along dimension 0
- grad_shift: float32 [4096], P('dp'), parts along dimension 0
There are 16 independent parts, one for each index of `dp`. A program takes and returns all parts, laid end to end along the dimension named above; an argument that names none is the same for every part. Nothing has to cross between parts.
All inputs are finite; a program needn't handle non-finite values.
Results may differ from a plain program's by a relative error of at most 0.009.
Values may be sent and summed in bfloat16 or wider, within the bound.
No kernel may reach another device: no remote copies, remote signals or barrier semaphores. Data moves between devices by JAX's collectives and lax.ppermute only.
A program may use at most 128 MiB of HBM per device.

v0:
```python
import jax
import jax.numpy as jnp
from jax import lax
from jax.sharding import PartitionSpec as P

C1 = 512
GROUPS = 32


epsilon = 1e-06


def copy_for_each(array, axis):
    devices = lax.axis_size(axis)
    return lax.all_to_all(
        jnp.broadcast_to(array[None], (devices, *array.shape)), axis, 0, 0, tiled=True
    )


def taken_together(array, axis):
    everything = copy_for_each(array, axis)
    return jnp.sum(everything, axis=0)


def packed_total(arrays, axis):
    ends = [0]
    for a in arrays:
        ends.append(ends[-1] + a.size)
    so_far = taken_together(jnp.concatenate([a.ravel() for a in arrays]), axis)
    return tuple((so_far[b:e].reshape(a.shape) for a, b, e in zip(arrays, ends, ends[1:])))


def shifted(block, axis, distance):
    devices = range(lax.axis_size(axis))
    route = [(i - distance, i) for i in devices if i - distance in devices]
    return lax.ppermute(block, axis, route)


def in_order(tiles, dim):
    tiles = jnp.moveaxis(tiles, 0, dim)
    shape = tiles.shape
    return tiles.reshape(*shape[:dim], shape[dim] * shape[dim + 1], *shape[dim + 2 :])


def gather_directly(array, axis, dim):
    tiles = copy_for_each(array, axis)
    return in_order(tiles, dim)


def extended_2(cells, sides, width):
    for axis, dim in sides:
        count = lax.axis_size(axis)
        ends = count - 1
        head = lax.slice_in_dim(cells, 0, width, axis=dim)
        tail = lax.slice_in_dim(cells, cells.shape[dim] - width, cells.shape[dim], axis=dim)
        cells = jnp.concatenate(
            [
                lax.ppermute(tail, axis, [(i, (i + 1) % count) for i in range(ends)]),
                cells,
                lax.ppermute(head, axis, [((i + 1) % count, i) for i in range(ends)]),
            ],
            axis=dim,
        )
    return cells


def gather_in_order(array, axes, turns):
    tiles = array
    for k in turns:
        tiles = lax.all_gather(tiles, axes[k])
    done = turns[::-1]
    back = [done.index(k) for k in range(len(axes))]
    tiles = tiles.transpose(*back, *range(len(axes), tiles.ndim))
    return tiles.reshape(-1, *array.shape)


def whole_of(array, axes, turns, dim):
    return in_order(gather_in_order(array, axes, turns), dim)


def cut_along(array, dim, devices):
    before, after = (array.shape[:dim], array.shape[dim + 1 :])
    return jnp.moveaxis(array.reshape(*before, devices, -1, *after), dim, 0)


def sum_at_owner(array, axis, dim):
    tiles = cut_along(array, dim, lax.axis_size(axis))
    arrived = lax.all_to_all(tiles, axis, split_axis=0, concat_axis=0, tiled=True)
    return arrived.sum(axis=0)


def standardize(values, mean_value, inverse, groups):
    shape_full = values.shape
    grouped = values.reshape(shape_full[:-1] + (groups, shape_full[-1] // groups))
    return ((grouped - mean_value[:, None]) * inverse[:, None]).reshape(shape_full)


def causal_taps(padded, weight, frames, rows, cols):
    channels_in = padded.shape[-1]
    summed = jnp.zeros((frames * rows * cols, weight.shape[1]), jnp.float32)
    for lag_step in range(3):
        for row_step in range(3):
            for col_step in range(3):
                tap_index = (lag_step * 3 + row_step) * 3 + col_step
                window = padded[
                    lag_step : lag_step + frames,
                    row_step : row_step + rows,
                    col_step : col_step + cols,
                ]
                kernel = weight[tap_index * channels_in : (tap_index + 1) * channels_in]
                summed = summed + jnp.dot(
                    window.reshape(-1, channels_in), kernel, preferred_element_type=jnp.float32
                )
    return summed.reshape(frames, rows, cols, weight.shape[1])


def transposed_taps(padded, weight, frames, rows, cols):
    channels_out = padded.shape[-1]
    channels_in = weight.shape[0] // 27
    summed = jnp.zeros((frames * rows * cols, channels_in), jnp.float32)
    for lag_step in range(3):
        for row_step in range(3):
            for col_step in range(3):
                tap_index = (lag_step * 3 + row_step) * 3 + col_step
                window = padded[
                    2 - lag_step : 2 - lag_step + frames,
                    2 - row_step : 2 - row_step + rows,
                    2 - col_step : 2 - col_step + cols,
                ]
                kernel = weight[tap_index * channels_in : (tap_index + 1) * channels_in]
                summed = summed + lax.dot_general(
                    window.reshape(-1, channels_out),
                    kernel,
                    (((1,), (1,)), ((), ())),
                    preferred_element_type=jnp.float32,
                )
    return summed.reshape(frames, rows, cols, channels_in)


def weight_terms(padded, grads, frames, rows, cols):
    channels_in = padded.shape[-1]
    flat_grads = grads.reshape(-1, grads.shape[-1])
    blocks = []
    for row_step in range(3):
        for col_step in range(3):
            window = padded[2 : 2 + frames, row_step : row_step + rows, col_step : col_step + cols]
            blocks.append(
                lax.dot_general(
                    window.reshape(-1, channels_in),
                    flat_grads,
                    (((0,), (0,)), ((), ())),
                    preferred_element_type=jnp.float32,
                )
            )
    return jnp.concatenate(blocks, 0)


def local(
    latent,
    gain_latent,
    shift_latent,
    conv_latent,
    up_weight,
    gain_block,
    shift_block,
    conv_block,
    cotangent,
):
    per_group = C1 // GROUPS
    groups_here = latent.shape[-1] // per_group
    latent_f32 = latent.astype(jnp.float32)
    grouped = latent_f32.reshape(-1, groups_here, per_group)
    first_sums = jnp.sum(grouped, axis=(0, 2))
    second_sums = jnp.sum(grouped * grouped, axis=(0, 2))
    first_totals, second_totals = packed_total((first_sums, second_sums), "tm")
    count_latent = grouped.shape[0] * per_group * lax.axis_size("tm")
    mean_latent = first_totals / count_latent
    inverse_latent = lax.rsqrt(second_totals / count_latent - mean_latent * mean_latent + epsilon)
    normed = (
        standardize(latent_f32, mean_latent, inverse_latent, groups_here) * gain_latent
        + shift_latent
    )
    active = jax.nn.silu(normed).astype(jnp.bfloat16)
    earlier = shifted(active, "tm", 1)
    extended = jnp.concatenate([earlier, active], 0)
    all_channels = gather_directly(extended, "height", 3)
    padded = jnp.pad(all_channels, ((0, 0), (1, 1), (1, 1), (0, 0)))
    latent_weight = lax.all_gather(conv_latent, "tm", axis=0, tiled=True)
    frames_latent, rows_latent, cols_latent = (latent.shape[0], latent.shape[1], latent.shape[2])
    mixed = causal_taps(padded, latent_weight, frames_latent, rows_latent, cols_latent)
    refined = (latent_f32 + mixed).astype(jnp.bfloat16)
    band_rows = rows_latent // lax.axis_size("height")
    own_band = lax.all_to_all(refined, "height", split_axis=1, concat_axis=3, tiled=True)
    flat_band = own_band.reshape(-1, own_band.shape[-1])
    expanded = jnp.dot(
        flat_band, gather_directly(up_weight, "height", 0), preferred_element_type=jnp.float32
    )
    channels_block = up_weight.shape[1] // 8
    spread = expanded.reshape(frames_latent, band_rows, cols_latent, 2, 2, 2, channels_block)
    spread = spread.transpose(0, 3, 1, 4, 2, 5, 6)
    upsampled = spread.reshape(
        2 * frames_latent, 2 * band_rows, 2 * cols_latent, channels_block
    ).astype(jnp.bfloat16)
    frames_block, rows_block, cols_block = (
        upsampled.shape[0],
        upsampled.shape[1],
        upsampled.shape[2],
    )
    up_f32 = upsampled.astype(jnp.float32)
    per_block = channels_block // GROUPS
    grouped_block = up_f32.reshape(-1, GROUPS, per_block)
    block_first = jnp.sum(grouped_block, axis=(0, 2))
    block_second = jnp.sum(grouped_block * grouped_block, axis=(0, 2))
    block_first, block_second = packed_total((block_first, block_second), ("tm", "height"))
    count_block = grouped_block.shape[0] * per_block * lax.axis_size("tm") * lax.axis_size("height")
    mean_block = block_first / count_block
    inverse_block = lax.rsqrt(block_second / count_block - mean_block * mean_block + epsilon)
    standard = standardize(up_f32, mean_block, inverse_block, GROUPS)
    normed_block = standard * gain_block + shift_block
    active_block = jax.nn.silu(normed_block).astype(jnp.bfloat16)
    before = shifted(active_block[-2:], "tm", 1)
    ext_block = jnp.concatenate([before, active_block], 0)
    beside_all = extended_2(ext_block, (("height", 1),), 1)
    padded_block = jnp.pad(beside_all, ((0, 0), (0, 0), (1, 1), (0, 0)))
    block_weight = whole_of(conv_block, ("tm", "height"), (0, 1), 0)
    mixed_block = causal_taps(padded_block, block_weight, frames_block, rows_block, cols_block)
    decoded = (up_f32 + mixed_block).astype(jnp.bfloat16)
    after = shifted(cotangent[:2], "tm", -1)
    grad_ext = jnp.concatenate([cotangent, after], 0)
    grad_around = extended_2(grad_ext, (("height", 1),), 1)
    grad_padded = jnp.pad(grad_around, ((0, 0), (0, 0), (1, 1), (0, 0)))
    grad_active = transposed_taps(grad_padded, block_weight, frames_block, rows_block, cols_block)
    local_terms = weight_terms(padded_block, cotangent, frames_block, rows_block, cols_block)
    time_summed = sum_at_owner(local_terms, "tm", 0)
    grad_weight = sum_at_owner(time_summed, "height", 0)
    sigmoid = jax.nn.sigmoid(normed_block)
    grad_normed = grad_active * sigmoid * (1.0 + normed_block * (1.0 - sigmoid))
    flat_grad = grad_normed.reshape(-1, channels_block)
    flat_standard = standard.reshape(-1, channels_block)
    grad_shift, grad_gain = packed_total(
        (jnp.sum(flat_grad, axis=0), jnp.sum(flat_grad * flat_standard, axis=0)), ("tm", "height")
    )
    first_mean = jnp.sum((gain_block * grad_shift).reshape(GROUPS, per_block), axis=1) / count_block
    second_mean = jnp.sum((gain_block * grad_gain).reshape(GROUPS, per_block), axis=1) / count_block
    grouped_grad = (grad_normed * gain_block).reshape(-1, GROUPS, per_block)
    grouped_standard = standard.reshape(-1, GROUPS, per_block)
    corrected = (
        grouped_grad - first_mean[:, None] - grouped_standard * second_mean[:, None]
    ) * inverse_block[:, None]
    grad_upsampled = (cotangent.astype(jnp.float32) + corrected.reshape(cotangent.shape)).astype(
        jnp.bfloat16
    )
    return (decoded, grad_upsampled, grad_weight, grad_gain, grad_shift)


def solution(mesh):
    return jax.shard_map(
        local,
        mesh=mesh,
        in_specs=(
            P(("dp", "tm"), None, None, "height"),
            P("height"),
            P("height"),
            P("tm", "height"),
            P("height", None),
            P(),
            P(),
            P(("tm", "height"), None),
            P(("dp", "tm"), "height", None, None),
        ),
        out_specs=(
            P(("dp", "tm"), "height", None, None),
            P(("dp", "tm"), "height", None, None),
            P(("dp", "tm", "height"), None),
            P("dp"),
            P("dp"),
        ),
        check_vma=False,
    )
```

profile of v0, /device:TPU:2, one launch (start us, length us, event | category | flops | bytes accessed | tf_op | source)
XLA Modules:
  0.0 456.5 jit_solution(3244054950084139941)
XLA Ops:
  7.2 54.2 %all-gather = bf16[1728,256]{1,0:T(8,128)(2,1)} all-gather(bf16[216,256]{1,0:T(8,128)(2,1)} %param.16), channel_id=2, replica_groups=mesh['dp'=16,'tm'=8,'height'=4] {'tm'}, dimensions={0}, use_global_device_ids=true | all-gather | bytes 995328 | tf_op jit(solution)/shard_map/all_gather | solution.py:70
  63.4 10.3 %all-to-all-start = ((f32[8,1,16]{2,1,0:T(1,128)}), f32[8,1,16]{2,1,0:T(1,128)S(1)}, u32[]{:S(2)}, u32[]{:S(2)}) async-start(f32[8,1,16]{2,1,0:T(1,128)} %broadcast_in_dim.10), calls=%async_computation | async-start | bytes 8192 | tf_op jit(solution)/shard_map/all_to_all | solution.py:15
  75.9 8.1 %all-to-all-done = f32[8,1,16]{2,1,0:T(1,128)S(1)} async-done(((f32[8,1,16]{2,1,0:T(1,128)}), f32[8,1,16]{2,1,0:T(1,128)S(1)}, u32[]{:S(2)}, u32[]{:S(2)}) %all-to-all-start) | async-done | bytes 544 | tf_op jit(solution)/shard_map/all_to_all | solution.py:15
  85.3 2.5 collective-permute-start
  90.7 4.5 all-to-all-start.1
  96.5 4.6 collective-permute-start.5
  101.4 8.3 %all-to-all-done.1 = bf16[4,4,8,16,128]{4,3,2,1,0:T(8,128)(2,1)S(1)} async-done(((bf16[4,4,8,16,128]{4,3,2,1,0:T(8,128)(2,1)}), bf16[4,4,8,16,128]{4,3,2,1,0:T(8,128)(2,1)S(1)}, u32[]{:S(2)}, u32[]{:S(2)}) %all-to-all-start.1) | async-done | bytes 524320 | tf_op jit(solution)/shard_map/all_to_all | solution.py:15
  111.3 3.6 all-to-all-start.3
  123.1 2.4 pad_slice_fusion
  125.4 19.1 %all-to-all-done.3 = bf16[4,128,2048]{1,2,0:T(8,128)(2,1)S(1)} async-done(((bf16[4,128,2048]{1,2,0:T(8,128)(2,1)}), bf16[4,128,2048]{1,2,0:T(8,128)(2,1)S(1)}, u32[]{:S(2)}, u32[]{:S(2)}) %all-to-all-start.3) | async-done | bytes 2097184 | tf_op jit(solution)/shard_map/all_to_all | solution.py:15
  144.5 2.6 copy.75
  147.2 3.9 copy.76
  151.1 2.4 copy.79
  161.2 68.7 %all-gather.5.cloned.1.call-done = bf16[13824,128]{1,0:T(8,128)(2,1)} async-done(((bf16[1728,128]{1,0:T(8,128)(2,1)}), bf16[13824,128]{1,0:T(8,128)(2,1)}) %all-gather.5.cloned.1.call-update) | async-done | bytes 3538960 | tf_op jit(solution)/shard_map/all_gather | solution.py:188
  245.2 4.2 all-to-all-start.2
  251.6 3.6 all-to-all-done.2
  258.2 3.7 fusion.146
  266.1 4.8 %all-to-all-start.4 = ((f32[32,1,64]{2,1,0:T(1,128)}), f32[32,1,64]{2,1,0:T(1,128)S(1)}, u32[]{:S(2)}, u32[]{:S(2)}) async-start(f32[32,1,64]{2,1,0:T(1,128)} %broadcast_in_dim.13), calls=%async_computation.4 | async-start | bytes 32768 | tf_op jit(solution)/shard_map/all_to_all | solution.py:15
  272.9 2.2 copy.77
  275.2 2.2 reshape.485
  277.4 5.9 %all-to-all-done.4 = f32[32,1,64]{2,1,0:T(1,128)S(1)} async-done(((f32[32,1,64]{2,1,0:T(1,128)}), f32[32,1,64]{2,1,0:T(1,128)S(1)}, u32[]{:S(2)}, u32[]{:S(2)}) %all-to-all-start.4) | async-done | bytes 8224 | tf_op jit(solution)/shard_map/all_to_all | solution.py:15
  287.1 2.8 fusion.145
  290.6 6.5 %all-to-all-start.5 = ((f32[32,1,512]{2,1,0:T(1,128)}), f32[32,1,512]{2,1,0:T(1,128)S(1)}, u32[]{:S(2)}, u32[]{:S(2)}) async-start(f32[32,1,512]{2,1,0:T(1,128)} %broadcast_in_dim.14), calls=%async_computation.5 | async-start | bytes 131072 | tf_op jit(solution)/shard_map/all_to_all | solution.py:15
  298.5 11.5 %all-to-all-done.5 = f32[32,1,512]{2,1,0:T(1,128)S(1)} async-done(((f32[32,1,512]{2,1,0:T(1,128)}), f32[32,1,512]{2,1,0:T(1,128)S(1)}, u32[]{:S(2)}, u32[]{:S(2)}) %all-to-all-start.5) | async-done | bytes 65568 | tf_op jit(solution)/shard_map/all_to_all | solution.py:15
  311.4 2.2 add_convert_fusion
  313.6 2.3 collective-permute-start.1
  315.9 2.5 collective-permute-done.1
  319.8 4.6 collective-permute-start.2
  330.8 5.2 %all-to-all-start.6 = ((f32[8,288,256]{2,1,0:T(8,128)}), f32[8,288,256]{2,1,0:T(8,128)S(1)}, u32[]{:S(2)}, u32[]{:S(2)}) async-start(f32[8,288,256]{2,1,0:T(8,128)} %bitcast.329), calls=%async_computation.6 | async-start | bytes 4718592 | tf_op jit(solution)/shard_map/all_to_all | solution.py:88
  345.7 91.6 %all-to-all-done.6 = f32[8,288,256]{2,1,0:T(8,128)S(1)} async-done(((f32[8,288,256]{2,1,0:T(8,128)}), f32[8,288,256]{2,1,0:T(8,128)S(1)}, u32[]{:S(2)}, u32[]{:S(2)}) %all-to-all-start.6) | async-done | bytes 2359328 | tf_op jit(solution)/shard_map/all_to_all | solution.py:88
  438.2 4.0 all-to-all-start.7
  443.0 6.1 %all-to-all-done.7 = f32[4,72,256]{2,1,0:T(8,128)S(1)} async-done(((f32[4,72,256]{2,1,0:T(8,128)}), f32[4,72,256]{2,1,0:T(8,128)S(1)}, u32[]{:S(2)}, u32[]{:S(2)}) %all-to-all-start.7) | async-done | bytes 294944 | tf_op jit(solution)/shard_map/all_to_all | solution.py:88
  (297 shorter events, 80.0 us)
Async XLA Ops:
  7.2 93.9 %copy-start.53 = (bf16[128,2048]{1,0:T(8,128)(2,1)S(1)}, bf16[128,2048]{1,0:T(8,128)(2,1)}, u32[]{:S(2)}) copy-start(bf16[128,2048]{1,0:T(8,128)(2,1)} %param.13) | copy-start | bytes 1572868
  7.2 143.9 %all-gather.7.cloned.1.call-start = ((), (), s32[]{:S(2)}) async-start(), calls=%async_computation.9 | async-start | bytes 4423680 | tf_op jit(solution)/shard_map/all_gather | solution.py:70
  63.4 20.6 %all-to-all-start = ((f32[8,1,16]{2,1,0:T(1,128)}), f32[8,1,16]{2,1,0:T(1,128)S(1)}, u32[]{:S(2)}, u32[]{:S(2)}) async-start(f32[8,1,16]{2,1,0:T(1,128)} %broadcast_in_dim.10), calls=%async_computation | async-start | bytes 8192 | tf_op jit(solution)/shard_map/all_to_all | solution.py:15
  74.6 20.5 %collective-permute-start.4 = (bf16[2,4,32,256]{3,2,1,0:T(8,128)(2,1)S(1)}, bf16[2,4,32,256]{3,2,1,0:T(8,128)(2,1)S(1)}, u32[]{:S(2)}, u32[]{:S(2)}) collective-permute-start(bf16[2,4,32,256]{3,2,1,0:T(8,128)(2,1)S(1)} %slice.629), channel_id=1, source_target_pairs={{4,0},{8,4},{12,8},{16,12},{20,16},{24,20},{28,24},{5,1},{9,5},{13... | collective-permute-start | bytes 393224 | tf_op jit(solution)/shard_map/ppermute | solution.py:36
  85.3 4.4 collective-permute-start
  90.7 18.9 %all-to-all-start.1 = ((bf16[4,4,8,16,128]{4,3,2,1,0:T(8,128)(2,1)}), bf16[4,4,8,16,128]{4,3,2,1,0:T(8,128)(2,1)S(1)}, u32[]{:S(2)}, u32[]{:S(2)}) async-start(bf16[4,4,8,16,128]{4,3,2,1,0:T(8,128)(2,1)} %broadcast_in_dim.11), calls=%async_computation.1 | async-start | bytes 1048576 | tf_op jit(solution)/shard_map/all_to_all | solution.py:15
  95.1 134.7 %all-gather.5.cloned.1.call-start = ((), (), s32[]{:S(2)}) async-start(), calls=%async_computation.8 | async-start | bytes 3981312 | tf_op jit(solution)/shard_map/all_gather | solution.py:188
  95.2 19.7 %collective-permute-start.6 = (bf16[6,1,32,256]{3,2,1,0:T(8,128)(2,1)S(1)}, bf16[6,1,32,256]{3,2,1,0:T(8,128)(2,1)S(1)}, u32[]{:S(2)}, u32[]{:S(2)}) collective-permute-start(bf16[6,1,32,256]{3,2,1,0:T(8,128)(2,1)S(1)} %get-tuple-element.98), channel_id=1, source_target_pairs={{1,0},{2,1},{3,2},{5,4},{6,5},{7,6},{9,8},{10,9},{11,10},{13,12},{... | collective-permute-start | bytes 294920 | tf_op jit(solution)/shard_map/ppermute | solution.py:60
  96.5 18.4 %collective-permute-start.5 = (bf16[6,1,32,256]{3,2,1,0:T(8,128)(2,1)S(1)}, bf16[6,1,32,256]{3,2,1,0:T(8,128)(2,1)S(1)}, u32[]{:S(2)}, u32[]{:S(2)}) collective-permute-start(bf16[6,1,32,256]{3,2,1,0:T(8,128)(2,1)S(1)} %get-tuple-element.97), channel_id=1, source_target_pairs={{0,1},{1,2},{2,3},{4,5},{5,6},{6,7},{8,9},{9,10},{10,11},{12,13},{... | collective-permute-start | bytes 294920 | tf_op jit(solution)/shard_map/ppermute | solution.py:58
  111.3 33.2 %all-to-all-start.3 = ((bf16[4,128,2048]{1,2,0:T(8,128)(2,1)}), bf16[4,128,2048]{1,2,0:T(8,128)(2,1)S(1)}, u32[]{:S(2)}, u32[]{:S(2)}) async-start(bf16[4,128,2048]{1,2,0:T(8,128)(2,1)} %broadcast_in_dim.12), calls=%async_computation.3 | async-start | bytes 4194304 | tf_op jit(solution)/shard_map/all_to_all | solution.py:15
  153.5 133.6 %copy-start = (bf16[8,4,216,256]{3,2,1,0:T(8,128)(2,1)}, bf16[8,4,216,256]{3,2,1,0:T(8,128)(2,1)S(1)}, u32[]{:S(2)}) copy-start(bf16[8,4,216,256]{3,2,1,0:T(8,128)(2,1)S(1)} %copy.79) | copy-start | bytes 10616836
  229.9 10.2 %copy-start.51 = (bf16[2,8,16,512]{3,2,1,0:T(8,128)(2,1)S(1)}, bf16[2,8,16,512]{3,2,1,0:T(8,128)(2,1)}, u32[]{:S(2)}) copy-start(bf16[2,8,16,512]{3,2,1,0:T(8,128)(2,1)} %get-tuple-element.60) | copy-start | bytes 786436
  229.9 10.4 %copy-start.50 = (bf16[2,8,16,512]{3,2,1,0:T(8,128)(2,1)S(1)}, bf16[2,8,16,512]{3,2,1,0:T(8,128)(2,1)}, u32[]{:S(2)}) copy-start(bf16[2,8,16,512]{3,2,1,0:T(8,128)(2,1)} %get-tuple-element.61) | copy-start | bytes 786436
  229.9 10.7 %copy-start.49 = (bf16[2,8,16,512]{3,2,1,0:T(8,128)(2,1)S(1)}, bf16[2,8,16,512]{3,2,1,0:T(8,128)(2,1)}, u32[]{:S(2)}) copy-start(bf16[2,8,16,512]{3,2,1,0:T(8,128)(2,1)} %get-tuple-element.62) | copy-start | bytes 786436
  229.9 10.9 %copy-start.48 = (bf16[2,8,16,512]{3,2,1,0:T(8,128)(2,1)S(1)}, bf16[2,8,16,512]{3,2,1,0:T(8,128)(2,1)}, u32[]{:S(2)}) copy-start(bf16[2,8,16,512]{3,2,1,0:T(8,128)(2,1)} %get-tuple-element.63) | copy-start | bytes 786436
  231.2 9.8 %copy-start.47 = (bf16[2,8,16,512]{3,2,1,0:T(8,128)(2,1)S(1)}, bf16[2,8,16,512]{3,2,1,0:T(8,128)(2,1)}, u32[]{:S(2)}) copy-start(bf16[2,8,16,512]{3,2,1,0:T(8,128)(2,1)} %get-tuple-element.64) | copy-start | bytes 786436
  232.6 8.7 %copy-start.22 = (bf16[2,8,16,4,128]{4,3,2,1,0:T(4,128)(2,1)S(1)}, bf16[2,8,16,4,128]{4,3,2,1,0:T(4,128)(2,1)}, u32[]{:S(2)}) copy-start(bf16[2,8,16,4,128]{4,3,2,1,0:T(4,128)(2,1)} %copy.70) | copy-start | bytes 786436
  245.2 10.0 %all-to-all-start.2 = ((bf16[2,8,16,128]{3,2,0,1:T(8,128)(2,1)}), bf16[2,8,16,128]{3,2,0,1:T(8,128)(2,1)}, u32[]{:S(2)}, u32[]{:S(2)}) async-start(bf16[2,8,16,128]{3,2,0,1:T(8,128)(2,1)} %fusion.45), calls=%async_computation.2 | async-start | bytes 131072 | tf_op jit(solution)/shard_map/all_to_all | solution.py:193
  266.1 17.1 %all-to-all-start.4 = ((f32[32,1,64]{2,1,0:T(1,128)}), f32[32,1,64]{2,1,0:T(1,128)S(1)}, u32[]{:S(2)}, u32[]{:S(2)}) async-start(f32[32,1,64]{2,1,0:T(1,128)} %broadcast_in_dim.13), calls=%async_computation.4 | async-start | bytes 32768 | tf_op jit(solution)/shard_map/all_to_all | solution.py:15
  287.1 22.9 %copy-start.57 = (f32[256]{0:T(256)S(1)}, f32[256]{0:T(256)}, u32[]{:S(2)}) copy-start(f32[256]{0:T(256)} %param.14) | copy-start | bytes 3076
  287.1 24.3 %copy-start.58 = (f32[256]{0:T(256)S(1)}, f32[256]{0:T(256)}, u32[]{:S(2)}) copy-start(f32[256]{0:T(256)} %mul.160) | copy-start | bytes 3076
  287.1 24.3 %copy-start.59 = (f32[256]{0:T(256)S(1)}, f32[256]{0:T(256)}, u32[]{:S(2)}) copy-start(f32[256]{0:T(256)} %sub.74) | copy-start | bytes 3076
  287.1 24.3 %copy-start.60 = (f32[256]{0:T(256)S(1)}, f32[256]{0:T(256)}, u32[]{:S(2)}) copy-start(f32[256]{0:T(256)} %param.15) | copy-start | bytes 3076
  289.9 37.0 %copy-start.8 = (bf16[4,4,32,256]{3,2,1,0:T(8,128)(2,1)S(1)}, bf16[4,4,32,256]{3,2,1,0:T(8,128)(2,1)}, u32[]{:S(2)}) copy-start(bf16[4,4,32,256]{3,2,1,0:T(8,128)(2,1)} %param.17) | copy-start | bytes 786436
  290.6 19.4 %all-to-all-start.5 = ((f32[32,1,512]{2,1,0:T(1,128)}), f32[32,1,512]{2,1,0:T(1,128)S(1)}, u32[]{:S(2)}, u32[]{:S(2)}) async-start(f32[32,1,512]{2,1,0:T(1,128)} %broadcast_in_dim.14), calls=%async_computation.5 | async-start | bytes 131072 | tf_op jit(solution)/shard_map/all_to_all | solution.py:15
  298.5 26.5 %copy-start.4 = (f32[4,4,32,256]{3,2,1,0:T(8,128)}, f32[4,4,32,256]{3,2,1,0:T(8,128)S(1)}, u32[]{:S(2)}) copy-start(f32[4,4,32,256]{3,2,1,0:T(8,128)S(1)} %reshape.484) | copy-start | bytes 1572868
  313.6 4.8 %collective-permute-start.1 = (bf16[2,4,32,256]{3,2,1,0:T(8,128)(2,1)S(1)}, bf16[2,4,32,256]{3,2,1,0:T(8,128)(2,1)S(1)}, u32[]{:S(2)}, u32[]{:S(2)}) collective-permute-start(bf16[2,4,32,256]{3,2,1,0:T(8,128)(2,1)S(1)} %slice.690), channel_id=1, source_target_pairs={{0,4},{4,8},{8,12},{12,16},{16,20},{20,24},{24,28},{1,5},{5,9},{9,... | collective-permute-start | bytes 393224 | tf_op jit(solution)/shard_map/ppermute | solution.py:36
  318.5 6.5 %collective-permute-start.3 = (bf16[6,1,32,256]{3,2,1,0:T(8,128)(2,1)S(1)}, bf16[6,1,32,256]{3,2,1,0:T(8,128)(2,1)S(1)}, u32[]{:S(2)}, u32[]{:S(2)}) collective-permute-start(bf16[6,1,32,256]{3,2,1,0:T(8,128)(2,1)S(1)} %get-tuple-element.104), channel_id=1, source_target_pairs={{1,0},{2,1},{3,2},{5,4},{6,5},{7,6},{9,8},{10,9},{11,10},{13,12},{... | collective-permute-start | bytes 294920 | tf_op jit(solution)/shard_map/ppermute | solution.py:60
  319.8 6.8 %collective-permute-start.2 = (bf16[6,1,32,256]{3,2,1,0:T(8,128)(2,1)S(1)}, bf16[6,1,32,256]{3,2,1,0:T(8,128)(2,1)S(1)}, u32[]{:S(2)}, u32[]{:S(2)}) collective-permute-start(bf16[6,1,32,256]{3,2,1,0:T(8,128)(2,1)S(1)} %get-tuple-element.103), channel_id=1, source_target_pairs={{0,1},{1,2},{2,3},{4,5},{5,6},{6,7},{8,9},{9,10},{10,11},{12,13},{... | collective-permute-start | bytes 294920 | tf_op jit(solution)/shard_map/ppermute | solution.py:58
  330.8 106.5 %all-to-all-start.6 = ((f32[8,288,256]{2,1,0:T(8,128)}), f32[8,288,256]{2,1,0:T(8,128)S(1)}, u32[]{:S(2)}, u32[]{:S(2)}) async-start(f32[8,288,256]{2,1,0:T(8,128)} %bitcast.329), calls=%async_computation.6 | async-start | bytes 4718592 | tf_op jit(solution)/shard_map/all_to_all | solution.py:88
  345.0 97.2 %copy-start.5 = (f32[4,4,32,256]{3,2,1,0:T(8,128)S(1)}, f32[4,4,32,256]{3,2,1,0:T(8,128)}, u32[]{:S(2)}) copy-start(f32[4,4,32,256]{3,2,1,0:T(8,128)} %copy-done.4) | copy-start | bytes 1572868
  438.2 10.8 %all-to-all-start.7 = ((f32[4,72,256]{2,1,0:T(8,128)}), f32[4,72,256]{2,1,0:T(8,128)S(1)}, u32[]{:S(2)}, u32[]{:S(2)}) async-start(f32[4,72,256]{2,1,0:T(8,128)} %bitcast.332), calls=%async_computation.7 | async-start | bytes 589824 | tf_op jit(solution)/shard_map/all_to_all | solution.py:88
  (46 other events, 112.8 us)
Sparse Core Ops, SparseCore 0:
  61.5 69.8 all-gather.6
  133.5 96.3 all-gather.4
where the time goes:
time: 458 us; the launch traced here: 457 us
  waiting for transfers between devices  228 us (50%)
  starting transfers between devices  60.9 us (13%)
  blocking collectives  54.2 us (12%)
  local copies, waits for them, and re-layouts  41.6 us (9%)
  matrix products  40.5 us (9%)
  between operations  15.6 us (3%)
  other arithmetic  15.3 us (3%)
    all_to_all x2, waiting for transfers between devices, sum_at_owner(): lax.all_to_all(tiles, axis, split_axis=0, concat_axis=0, tiled=True)  97.7 us
    all_gather x1, waiting for transfers between devices, local(): latent_weight = lax.all_gather(conv_latent, 'tm', axis=0, tiled=True)  68.7 us
    all_gather x1, blocking collectives, gather_in_order(): tiles = lax.all_gather(tiles, axes[k])  54.2 us
    all_to_all x5, waiting for transfers between devices, copy_for_each(): lax.all_to_all(jnp.broadcast_to(array[None], (devices, *array.shape)), ax...  52.8 us
    all_to_all x5, starting transfers between devices, copy_for_each(): lax.all_to_all(jnp.broadcast_to(array[None], (devices, *array.shape)), ax...  29.7 us
    dot_general x54, matrix products, causal_taps(): jnp.dot(window.reshape(-1, channels_in), kernel, preferred_element_type=j...  20.3 us
    dot_general x27, matrix products, transposed_taps(): lax.dot_general(window.reshape(-1, channels_out), kernel, (((1,), (1,)),...  14 us
    all_to_all x2, starting transfers between devices, sum_at_owner(): lax.all_to_all(tiles, axis, split_axis=0, concat_axis=0, tiled=True)  9.22 us
  transfers between devices with their start and end apart: 17, of which 13 were waited for; matrix products, arithmetic and copies ran while one was open for 12% of the time, Pallas kernels for 0%

commit v1 on v0

v1 whole, which is shorter than its diff:
```python
import jax
import jax.numpy as jnp
from jax import lax
from jax.experimental import pallas as pl
from jax.experimental.pallas import tpu as pltpu
from jax.sharding import Mesh, PartitionSpec as P

EPS = 1e-6
BF = jnp.bfloat16
F32 = jnp.float32
VM = pl.BlockSpec(memory_space=pltpu.VMEM)
SM = pl.BlockSpec(memory_space=pltpu.SMEM)
HB = pl.BlockSpec(memory_space=pl.ANY)
PARAMS = pltpu.CompilerParams(vmem_limit_bytes=50 * 1024 * 1024)


def dot(a, b, precision=None):
    return jnp.dot(a, b, preferred_element_type=F32, precision=precision)


def sigmoid(v):
    return 0.5 * jnp.tanh(0.5 * v) + 0.5


def group_matrix(channels, per_group):
    rows = lax.broadcasted_iota(jnp.int32, (channels, channels), 0) // per_group
    cols = lax.broadcasted_iota(jnp.int32, (channels, channels), 1) // per_group
    return jnp.where(rows == cols, 1.0, 0.0).astype(F32)


def group_sums(sums, per_group):
    return dot(sums, group_matrix(sums.shape[1], per_group), lax.Precision.HIGHEST)


def moved(v, step, cols=16):
    n = v.shape[0]
    col = lax.broadcasted_iota(jnp.int32, v.shape, 0) % cols
    if step < 0:
        return jnp.where(col == 0, 0.0, pltpu.roll(v, 1, 0))
    return jnp.where(col == cols - 1, 0.0, pltpu.roll(v, n - 1, 0))


def latent_sums_kernel(x_ref, gain_ref, shift_ref, out_ref):
    v = x_ref[...].reshape(-1, 128).astype(F32)
    rows = jnp.concatenate(
        [
            jnp.sum(v, axis=0, keepdims=True),
            jnp.sum(v * v, axis=0, keepdims=True),
            gain_ref[...],
            shift_ref[...],
            jnp.zeros((4, 128), F32),
        ],
        axis=0,
    )
    out_ref[...] = jnp.broadcast_to(rows[None], out_ref.shape)


def latent_conv_kernel(meta, lat_ref, stats_ref, mine, other, out_ref, act, w, sem):
    core, t, h = meta[0], meta[1], meta[2]

    def weight_copies(low, high):
        copies = []
        for xi in range(4):
            for ti in range(8):
                at = ti * 1728 + xi * 432
                copies.append(
                    pltpu.make_async_copy(
                        low.at[xi, ti, pl.ds(0, 208)], w.at[pl.ds(at, 208)], sem
                    )
                )
                copies.append(
                    pltpu.make_async_copy(high.at[xi, ti], w.at[pl.ds(at + 208, 224)], sem)
                )
        return copies

    @pl.when(core == 0)
    def _():
        for c in weight_copies(mine, other):
            c.start()

    @pl.when(core == 1)
    def _():
        for c in weight_copies(other, mine):
            c.start()

    frame = lax.broadcasted_iota(jnp.int32, (640, 128), 0) // 128
    inside = frame + 2 * t - 3 >= 0
    zero_row = jnp.zeros((5, 1, 16, 128), BF)
    for j in range(4):
        part = stats_ref[0, j]
        for k in range(1, 8):
            part = part + stats_ref[k, j]
        total = group_sums(part, 16) * (1.0 / 32768.0)
        mean = total[0:1]
        inverse = lax.rsqrt(total[1:2] - mean * mean + EPS)
        v = lat_ref[j].reshape(640, 128).astype(F32)
        normed = (v - mean) * inverse * stats_ref[0, j, 2:3] + stats_ref[0, j, 3:4]
        a = jnp.where(inside, normed * sigmoid(normed), 0.0)
        a = a.astype(BF).astype(F32)
        for dc in range(3):
            s = a if dc == 1 else moved(a, dc - 1)
            act[dc, :, 1:9, :, j * 128 : j * 128 + 128] = s.astype(BF).reshape(5, 8, 16, 128)
            act[dc, :, 0:1, :, j * 128 : j * 128 + 128] = zero_row
            act[dc, :, 9:10, :, j * 128 : j * 128 + 128] = zero_row

    for c in weight_copies(mine, other):
        c.wait()
    acc = lat_ref[h, 2:5].reshape(384, 128).astype(F32)
    total = None
    for lag in range(3):
        for dr in range(3):
            for dc in range(3):
                tap = (lag * 3 + dr) * 3 + dc
                window = act[dc, lag : lag + 3, dr : dr + 8].reshape(384, 512)
                term = dot(window, w[tap * 512 : tap * 512 + 512, :])
                total = term if total is None else total + term
    out_ref[...] = (acc + total).astype(BF).reshape(3, 8, 16, 128)


def upsample_kernel(meta, ref_ref, mine, other, up_ref, sums_ref, w, sem):
    core = meta[0]
    copies = []
    for j in range(4):
        copies.append(
            pltpu.make_async_copy(mine.at[j], w.at[pl.ds(j * 128 + core * 64, 64)], sem)
        )
        copies.append(
            pltpu.make_async_copy(
                other.at[j], w.at[pl.ds(j * 128 + (1 - core) * 64, 64)], sem
            )
        )
    for c in copies:
        c.start()
    for c in copies:
        c.wait()
    x = jnp.concatenate([ref_ref[j].reshape(384, 128) for j in range(4)], axis=1)
    first = jnp.zeros((1, 256), F32)
    second = jnp.zeros((1, 256), F32)
    for p in range(2):
        for q in range(2):
            for s in range(2):
                at = ((p * 2 + q) * 2 + s) * 256
                e = dot(x, w[:, at : at + 256]).astype(BF)
                up_ref[:, p, :, q, s] = e.reshape(3, 8, 16, 256)
                own = e[128:].astype(F32)
                first += jnp.sum(own, axis=0, keepdims=True)
                second += jnp.sum(own * own, axis=0, keepdims=True)
    rows = jnp.concatenate([first, second, jnp.zeros((6, 256), F32)], axis=0)
    sums_ref[...] = jnp.broadcast_to(rows[None], sums_ref.shape)


def grad_active_kernel(meta, cot_ref, w_ref, out_ref, q):
    h = meta[2]
    for row in range(6):
        block = jnp.clip(h + (row + 3) // 4 - 1, 0, 3)
        v = cot_ref[block, :, (row + 3) % 4]
        if row == 0:
            v = jnp.where(h > 0, v, jnp.zeros_like(v))
        if row == 5:
            v = jnp.where(h < 3, v, jnp.zeros_like(v))
        s0, s1 = v[:, 0], v[:, 1]
        q[:, row, 1] = s0
        q[:, row, 2] = s1
        q[:, row, 0] = moved(s1.reshape(96, 256).astype(F32), -1).astype(BF).reshape(6, 16, 256)
        q[:, row, 3] = moved(s0.reshape(96, 256).astype(F32), 1).astype(BF).reshape(6, 16, 256)
    total = None
    for lag in range(3):
        for dr in range(3):
            for dc in range(3):
                tap = (lag * 3 + dr) * 3 + dc
                window = q[2 - lag : 6 - lag, 2 - dr : 6 - dr, 2 - dc : 4 - dc].reshape(512, 256)
                term = lax.dot_general(
                    window,
                    w_ref[tap * 256 : tap * 256 + 256, :],
                    (((1,), (1,)), ((), ())),
                    preferred_element_type=F32,
                )
                total = term if total is None else total + term
    out_ref[...] = total


def block_moments(stats_ref):
    part = stats_ref[0]
    for k in range(1, 8):
        part = part + stats_ref[k]
    total = group_sums(part, 8) * (1.0 / 131072.0)
    mean = total[0:1]
    return mean, lax.rsqrt(total[1:2] - mean * mean + EPS)


def grad_norm_kernel(meta, up_ref, stats_ref, gain_ref, shift_ref, ga_ref, gn_ref, sums_ref):
    h = meta[2]
    mean, inverse = block_moments(stats_ref)
    own = up_ref[2:6, pl.ds(4 * h, 4)].reshape(512, 256).astype(F32)
    standard = (own - mean) * inverse
    normed = standard * gain_ref[...] + shift_ref[...]
    sigma = sigmoid(normed)
    gn = ga_ref[...] * sigma * (1.0 + normed * (1.0 - sigma))
    gn_ref[...] = gn
    rows = jnp.concatenate(
        [
            jnp.sum(gn, axis=0, keepdims=True),
            jnp.sum(gn * standard, axis=0, keepdims=True),
            jnp.zeros((6, 256), F32),
        ],
        axis=0,
    )
    sums_ref[...] = jnp.broadcast_to(rows[None], sums_ref.shape)


def weight_grad_kernel(
    meta, up_ref, stats_ref, gain_ref, shift_ref, cot_ref, gw_ref, q_ref, full
):
    t, h = meta[1], meta[2]
    mean, inverse = block_moments(stats_ref)
    scale = inverse * gain_ref[...]
    offset = shift_ref[...] - mean * scale
    q_ref[:, 0:1] = jnp.zeros((6, 1, 4, 16, 256), BF)
    q_ref[:, 17:18] = jnp.zeros((6, 1, 4, 16, 256), BF)
    for f in range(6):
        for s in range(2):
            v = up_ref[f, :, s].reshape(256, 256).astype(F32)
            normed = v * scale + offset
            a = normed * sigmoid(normed)
            if f < 2:
                a = jnp.where(t > 0, a, 0.0)
            a = a.astype(BF)
            a32 = a.astype(F32)
            q_ref[f, 1:17, 1 + s] = a.reshape(16, 16, 256)
            side = moved(a32, 1 if s == 0 else -1).astype(BF).reshape(16, 16, 256)
            q_ref[f, 1:17, 3 if s == 0 else 0] = side
    for dr in range(3):
        for dc in range(3):
            window = q_ref[2:6, dr : dr + 16, dc : dc + 2].reshape(2048, 256)
            g = dot(cot_ref[...], window)
            at = (dr * 3 + dc) * 256
            full[at : at + 256, :] = g.T
    for k in range(8):
        gw_ref[k] = full[pl.ds(pl.multiple_of(k * 288 + h * 72, 8), 72), :].astype(BF)


def interleave(scratch, v):
    for half in range(2):
        for s in range(2):
            part = v[:, s, :, half * 128 : half * 128 + 128]
            scratch[half, :, pl.ds(s, 16, stride=2), :] = part
    return jnp.concatenate([scratch[0], scratch[1]], axis=-1)


def decode_kernel(meta, up_ref, q_ref, w_ref, out_ref, scratch):
    h = meta[2]
    total = up_ref[2:6, pl.ds(4 * h, 4)].reshape(512, 256).astype(F32)
    conv = None
    for lag in range(3):
        for dr in range(3):
            for dc in range(3):
                tap = (lag * 3 + dr) * 3 + dc
                window = q_ref[lag : lag + 4, pl.ds(4 * h + dr, 4), dc : dc + 2].reshape(512, 256)
                term = dot(window, w_ref[tap * 256 : tap * 256 + 256, :])
                conv = term if conv is None else conv + term
    mixed = interleave(scratch, (total + conv).reshape(16, 2, 16, 256))
    out_ref[...] = mixed.astype(BF).reshape(4, 4, 32, 256)


def final_kernel(
    meta, up_ref, stats_ref, gain_ref, sums_ref, gn_ref, cot_ref, out_ref, totals_ref, scratch
):
    h = meta[2]
    mean, inverse = block_moments(stats_ref)
    total = sums_ref[0]
    for k in range(1, 32):
        total = total + sums_ref[k]
    totals_ref[...] = total
    gain = gain_ref[...]
    means = group_sums(total * gain, 8) * (1.0 / 131072.0)
    own = up_ref[2:6, pl.ds(4 * h, 4)].reshape(512, 256).astype(F32)
    standard = (own - mean) * inverse
    corrected = (gn_ref[...] * gain - means[0:1] - standard * means[1:2]) * inverse
    corrected = interleave(scratch, corrected.reshape(16, 2, 16, 256))
    cot = cot_ref[...].reshape(16, 32, 256).astype(F32)
    out_ref[...] = (cot + corrected).astype(BF).reshape(4, 4, 32, 256)


def gathered(v, axis, n):
    return lax.all_to_all(jnp.broadcast_to(v[None], (n, *v.shape)), axis, 0, 0, tiled=True)


def swapped(v):
    return lax.ppermute(v, "core", [(0, 1), (1, 0)])


def later(v, step):
    return lax.ppermute(v, "tm", [(i, i + step) for i in range(8) if 0 <= i + step < 8])


def struct(shape, dtype):
    return jax.ShapeDtypeStruct(shape, dtype)


def local(
    latent,
    gain_latent,
    shift_latent,
    conv_latent,
    up_weight,
    gain_block,
    shift_block,
    conv_block,
    cotangent,
):
    x, core = lax.axis_index("x"), lax.axis_index("core")
    t, h = lax.axis_index("tm"), lax.axis_index("height")
    meta = jnp.stack([core, t, h, x]).astype(jnp.int32)
    gain2, shift2 = gain_block[None], shift_block[None]

    piece = lax.dynamic_slice(conv_latent, (x * 432 + core * 208, 0), (224, 128))
    lat_w = gathered(gathered(piece, "tm", 8), "x", 4)
    lat_w_other = swapped(lat_w)

    sums = pl.pallas_call(
        latent_sums_kernel,
        out_shape=struct((32, 8, 128), F32),
        in_specs=[VM] * 3,
        out_specs=VM,
        compiler_params=PARAMS,
    )(latent, gain_latent[None], shift_latent[None])
    stats_latent = lax.all_to_all(sums, ("tm", "height"), 0, 0, tiled=True).reshape(8, 4, 8, 128)
    five = jnp.concatenate([later(latent[1:], 2), later(latent, 1), latent], 0)
    lat_all = gathered(five, "height", 4)

    up_piece = lax.dynamic_slice(up_weight, (core * 64, 0), (64, 2048))
    up_w = gathered(up_piece, "height", 4)
    up_w_other = swapped(up_w)

    refined = pl.pallas_call(
        latent_conv_kernel,
        out_shape=struct((3, 8, 16, 128), BF),
        in_specs=[SM, VM, VM, HB, HB],
        out_specs=VM,
        scratch_shapes=[
            pltpu.VMEM((3, 5, 10, 16, 512), BF),
            pltpu.VMEM((13824, 128), BF),
            pltpu.SemaphoreType.DMA,
        ],
        compiler_params=PARAMS,
    )(meta, lat_all, stats_latent, lat_w, lat_w_other)
    refined_all = gathered(refined, "height", 4)

    block_piece = lax.dynamic_slice(conv_block, (x * 54 + core * 27, 0), (27, 256))
    block_w = gathered(gathered(gathered(block_piece, "tm", 8), "height", 4), "x", 4)
    block_other = swapped(block_w)
    pair = jnp.where(core == 0, jnp.stack([block_w, block_other]), jnp.stack([block_other, block_w]))
    weight = pair.transpose(3, 2, 1, 0, 4, 5).reshape(6912, 256)

    phased = cotangent.reshape(4, 4, 16, 2, 256).transpose(0, 1, 3, 2, 4)
    six = jnp.concatenate([phased, later(phased[:2], -1)], 0)
    cot_all = gathered(six, "height", 4)
    cot_t = cot_all[:, :4].transpose(5, 1, 0, 2, 3, 4).reshape(256, 2048)
    grad_active = pl.pallas_call(
        grad_active_kernel,
        out_shape=struct((512, 256), F32),
        in_specs=[SM, VM, VM],
        out_specs=VM,
        scratch_shapes=[pltpu.VMEM((6, 6, 4, 16, 256), BF)],
        compiler_params=PARAMS,
    )(meta, cot_all, weight)

    up, up_sums = pl.pallas_call(
        upsample_kernel,
        out_shape=[struct((3, 2, 8, 2, 2, 16, 256), BF), struct((8, 8, 256), F32)],
        in_specs=[SM, VM, HB, HB],
        out_specs=[VM, VM],
        scratch_shapes=[pltpu.VMEM((512, 2048), BF), pltpu.SemaphoreType.DMA],
        compiler_params=PARAMS,
    )(meta, refined_all, up_w, up_w_other)
    up = up.reshape(6, 16, 2, 16, 256)
    stats_block = lax.all_to_all(up_sums, "tm", 0, 0, tiled=True)

    gn, grad_sums = pl.pallas_call(
        grad_norm_kernel,
        out_shape=[struct((512, 256), F32), struct((32, 8, 256), F32)],
        in_specs=[SM] + [VM] * 5,
        out_specs=[VM, VM],
        compiler_params=PARAMS,
    )(meta, up, stats_block, gain2, shift2, grad_active)
    all_sums = lax.all_to_all(grad_sums, ("tm", "height"), 0, 0, tiled=True)

    gw, q = pl.pallas_call(
        weight_grad_kernel,
        out_shape=[struct((8, 72, 256), BF), struct((6, 18, 4, 16, 256), BF)],
        in_specs=[SM] + [VM] * 5,
        out_specs=[VM, VM],
        scratch_shapes=[pltpu.VMEM((2304, 256), F32)],
        compiler_params=PARAMS,
    )(meta, up, stats_block, gain2, shift2, cot_t)
    gw_all = lax.all_to_all(gw, "tm", 0, 0, tiled=True)
    grad_weight = jnp.sum(gw_all.astype(F32), axis=0)

    decoded = pl.pallas_call(
        decode_kernel,
        out_shape=struct((4, 4, 32, 256), BF),
        in_specs=[SM] + [VM] * 3,
        out_specs=VM,
        scratch_shapes=[pltpu.VMEM((2, 16, 32, 128), F32)],
        compiler_params=PARAMS,
    )(meta, up, q, weight)

    grad_up, totals = pl.pallas_call(
        final_kernel,
        out_shape=[struct((4, 4, 32, 256), BF), struct((8, 256), F32)],
        in_specs=[SM] + [VM] * 6,
        out_specs=[VM, VM],
        scratch_shapes=[pltpu.VMEM((2, 16, 32, 128), F32)],
        compiler_params=PARAMS,
    )(meta, up, stats_block, gain2, all_sums, gn, cotangent)
    return decoded, grad_up, grad_weight, totals[1], totals[0]


def solution(mesh):
    fine = Mesh(
        mesh.devices.reshape(4, 2, 2, 8, 4), ("x", "zh", "core", "tm", "height")
    )
    dp = ("x", "zh", "core")
    return jax.shard_map(
        local,
        mesh=fine,
        in_specs=(
            P((*dp, "tm"), None, None, "height"),
            P("height"),
            P("height"),
            P("tm", "height"),
            P("height", None),
            P(),
            P(),
            P(("tm", "height"), None),
            P((*dp, "tm"), "height", None, None),
        ),
        out_specs=(
            P((*dp, "tm"), "height", None, None),
            P((*dp, "tm"), "height", None, None),
            P((*dp, "tm", "height"), None),
            P(dp),
            P(dp),
        ),
        check_vma=False,
    )
```

time: 458 us -> 290 us (0.63)
  the two profiles are of different devices: /device:TPU:2 before, /device:TPU:32 now
where the time goes in v1:
time: 290 us; the launch traced here: 288 us
  starting transfers between devices  85.6 us (30%)
  waiting for transfers between devices  76.1 us (26%)
  blocking collectives  53.8 us (19%)
  local copies, waits for them, and re-layouts  33.8 us (12%)
  Pallas kernels  32.2 us (11%)
  other arithmetic  5.34 us (2%)
    all_to_all x2, blocking collectives, gathered(): lax.all_to_all(jnp.broadcast_to(v[None], (n, *v.shape)), axis, 0, 0, tile...  53.8 us
    all_to_all x7, waiting for transfers between devices, gathered(): lax.all_to_all(jnp.broadcast_to(v[None], (n, *v.shape)), axis, 0, 0, tile...  52.4 us
    all_to_all x7, starting transfers between devices, gathered(): lax.all_to_all(jnp.broadcast_to(v[None], (n, *v.shape)), axis, 0, 0, tile...  36.8 us
    ppermute x3, starting transfers between devices, later(): lax.ppermute(v, 'tm', [(i, i + step) for i in range(8) if 0 <= i + step <...  10.8 us
    all_to_all x1, starting transfers between devices, local(): all_sums = lax.all_to_all(grad_sums, ('tm', 'height'), 0, 0, tiled=True)  10.7 us
    broadcast_in_dim x9, local copies, waits for them, and re-layouts, gathered(): jnp.broadcast_to(v[None], (n, *v.shape))  8.43 us
    all_to_all x1, starting transfers between devices, local(): stats_block = lax.all_to_all(up_sums, 'tm', 0, 0, tiled=True)  8.05 us
    unnamed x40, local copies, waits for them, and re-layouts  7.9 us
  transfers between devices with their start and end apart: 17, of which 12 were waited for; matrix products, arithmetic and copies ran while one was open for 9% of the time, Pallas kernels for 11%

profile of v1, /device:TPU:32, one launch (start us, length us, event | category | flops | bytes accessed | tf_op | source)
XLA Modules:
  0.0 287.9 jit_solution(5770829162027072721)
XLA Ops:
  2.1 12.6 %all-to-all-start.8 = ((bf16[8,27,256]{2,1,0:T(8,128)(2,1)}), bf16[8,27,256]{2,1,0:T(8,128)(2,1)S(1)}, u32[]{:S(2)}, u32[]{:S(2)}) async-start(bf16[8,27,256]{2,1,0:T(8,128)(2,1)} %broadcast_in_dim.36), calls=%async_computation.8 | async-start | bytes 262144 | tf_op jit(solution)/shard_map/all_to_all | solution.py:285
  17.6 8.3 %all-to-all-done.8 = bf16[8,27,256]{2,1,0:T(8,128)(2,1)S(1)} async-done(((bf16[8,27,256]{2,1,0:T(8,128)(2,1)}), bf16[8,27,256]{2,1,0:T(8,128)(2,1)S(1)}, u32[]{:S(2)}, u32[]{:S(2)}) %all-to-all-start.8) | async-done | bytes 110624 | tf_op jit(solution)/shard_map/all_to_all | solution.py:285
  25.9 7.9 %all-to-all-start.1 = ((f32[32,8,128]{2,1,0:T(8,128)}), f32[32,8,128]{2,1,0:T(8,128)S(1)}, u32[]{:S(2)}, u32[]{:S(2)}) async-start(f32[32,8,128]{2,1,0:T(8,128)} %shard_map.128), calls=%async_computation.1 | async-start | bytes 262144 | tf_op jit(solution)/shard_map/all_to_all | solution.py:327
  33.8 3.4 %collective-permute-start.1 = (bf16[2,8,16,128]{3,2,1,0:T(8,128)(2,1)}, bf16[2,8,16,128]{3,2,1,0:T(8,128)(2,1)S(1)}, u32[]{:S(2)}, u32[]{:S(2)}) collective-permute-start(bf16[2,8,16,128]{3,2,1,0:T(8,128)(2,1)} %x_ref.1), channel_id=1, source_target_pairs={{0,4},{4,8},{8,12},{12,16},{16,20},{20,24},{24,28},{1,5},{5,9},{9,... | collective-permute-start | bytes 196616 | tf_op jit(solution)/shard_map/ppermute | solution.py:293
  37.9 5.5 %collective-permute-start = (bf16[1,8,16,128]{3,2,1,0:T(8,128)(2,1)S(1)}, bf16[1,8,16,128]{3,2,1,0:T(8,128)(2,1)S(1)}, u32[]{:S(2)}, u32[]{:S(2)}) collective-permute-start(bf16[1,8,16,128]{3,2,1,0:T(8,128)(2,1)S(1)} %slice.15), channel_id=1, source_target_pairs={{0,8},{4,12},{8,16},{12,20},{16,24},{20,28},{1,9},{5,13},{9,17},{1... | collective-permute-start | bytes 98312 | tf_op jit(solution)/shard_map/ppermute | solution.py:293
  47.6 3.6 %all-to-all-start = ((bf16[4,5,8,16,128]{4,3,2,1,0:T(8,128)(2,1)}), bf16[4,5,8,16,128]{4,3,2,1,0:T(8,128)(2,1)S(1)}, u32[]{:S(2)}, u32[]{:S(2)}) async-start(bf16[4,5,8,16,128]{4,3,2,1,0:T(8,128)(2,1)} %broadcast_in_dim.26), calls=%async_computation | async-start | bytes 1310720 | tf_op jit(solution)/shard_map/all_to_all | solution.py:285
  51.2 8.8 %all-to-all-done.lat_ref = bf16[4,5,8,16,128]{4,3,2,1,0:T(8,128)(2,1)S(1)} async-done(((bf16[4,5,8,16,128]{4,3,2,1,0:T(8,128)(2,1)}), bf16[4,5,8,16,128]{4,3,2,1,0:T(8,128)(2,1)S(1)}, u32[]{:S(2)}, u32[]{:S(2)}) %all-to-all-start) | async-done | bytes 655392 | tf_op jit(solution)/shard_map/all_to_all | solution.py:285
  60.9 3.5 %all-to-all-start.9 = ((bf16[4,8,27,256]{3,1,2,0:T(8,128)(2,1)}), bf16[4,8,27,256]{3,1,2,0:T(8,128)(2,1)S(1)}, u32[]{:S(2)}, u32[]{:S(2)}) async-start(bf16[4,8,27,256]{3,1,2,0:T(8,128)(2,1)} %broadcast_in_dim.37), calls=%async_computation.9 | async-start | bytes 884736 | tf_op jit(solution)/shard_map/all_to_all | solution.py:285
  65.2 6.8 %all-to-all-done.9 = bf16[4,8,27,256]{3,1,2,0:T(8,128)(2,1)S(1)} async-done(((bf16[4,8,27,256]{3,1,2,0:T(8,128)(2,1)}), bf16[4,8,27,256]{3,1,2,0:T(8,128)(2,1)S(1)}, u32[]{:S(2)}, u32[]{:S(2)}) %all-to-all-start.9) | async-done | bytes 442400 | tf_op jit(solution)/shard_map/all_to_all | solution.py:285
  72.0 28.1 %all_to_all.65 = bf16[8,224,128]{2,1,0:T(8,128)(2,1)S(1)} all-to-all(bf16[8,224,128]{2,1,0:T(8,128)(2,1)S(1)} %broadcast_in_dim.29), channel_id=1, replica_groups=mesh['x'=4,'zh'=2,'core'=2,'tm'=8,'height'=4] {'tm'}, dimensions={0} | all-to-all | bytes 917504 | tf_op jit(solution)/shard_map/all_to_all | solution.py:285
  100.4 25.7 %all_to_all.66.mine = bf16[4,8,224,128]{3,2,1,0:T(8,128)(2,1)S(1)} all-to-all(bf16[4,8,224,128]{3,2,1,0:T(8,128)(2,1)S(1)} %broadcast_in_dim.30), channel_id=1, replica_groups=mesh['x'=4,'zh'=2,'core'=2,'tm'=8,'height'=4] {'x'}, dimensions={0} | all-to-all | bytes 3670016 | tf_op jit(solution)/shard_map/all_to_all | solution.py:285
  127.5 4.4 %all-to-all-start.10 = ((bf16[4,4,8,27,256]{4,2,3,1,0:T(8,128)(2,1)}), bf16[4,4,8,27,256]{4,2,3,1,0:T(8,128)(2,1)}, u32[]{:S(2)}, u32[]{:S(2)}) async-start(bf16[4,4,8,27,256]{4,2,3,1,0:T(8,128)(2,1)} %broadcast_in_dim.38), calls=%async_computation.10 | async-start | bytes 3538944 | tf_op jit(solution)/shard_map/all_to_all | solution.py:285
  133.9 17.9 %all-to-all-done.10 = bf16[4,4,8,27,256]{4,2,3,1,0:T(8,128)(2,1)} async-done(((bf16[4,4,8,27,256]{4,2,3,1,0:T(8,128)(2,1)}), bf16[4,4,8,27,256]{4,2,3,1,0:T(8,128)(2,1)}, u32[]{:S(2)}, u32[]{:S(2)}) %all-to-all-start.10) | async-done | bytes 1769504 | tf_op jit(solution)/shard_map/all_to_all | solution.py:285
  152.9 3.5 %all-to-all-start.5 = ((bf16[4,64,2048]{2,1,0:T(8,128)(2,1)}), bf16[4,64,2048]{2,1,0:T(8,128)(2,1)S(1)}, u32[]{:S(2)}, u32[]{:S(2)}) async-start(bf16[4,64,2048]{2,1,0:T(8,128)(2,1)} %broadcast_in_dim.32), calls=%async_computation.5 | async-start | bytes 2097152 | tf_op jit(solution)/shard_map/all_to_all | solution.py:285
  159.5 7.4 %shard_map.129 = bf16[3,8,16,128]{3,2,1,0:T(8,128)(2,1)S(1)} custom-call(s32[4]{0:T(128)S(1)} %pad_add_fusion.meta, bf16[4,5,8,16,128]{4,3,2,1,0:T(8,128)(2,1)S(1)} %copy-done.5, f32[8,4,8,128]{3,2,1,0:T(8,128)S(1)} %bitcast.28, bf16[4,8,224,128]{3,2,1,0:T(8,128)(2,1)S(1)} %all_to_all.66.mine, bf16[4,8,224,128]{3,2,1,0:T(8,128)(2,1)} %collective-permute-done.2.other), custom_call_target="tpu_custom_call" | custom-call | tf_op jit(solution)/shard_map/pallas_call | solution.py:335
  169.3 4.7 %all-to-all-start.4 = ((bf16[4,3,8,16,128]{4,3,2,1,0:T(8,128)(2,1)}), bf16[4,3,8,16,128]{4,3,2,1,0:T(8,128)(2,1)S(1)}, u32[]{:S(2)}, u32[]{:S(2)}) async-start(bf16[4,3,8,16,128]{4,3,2,1,0:T(8,128)(2,1)} %broadcast_in_dim.31), calls=%async_computation.4 | async-start | bytes 786432 | tf_op jit(solution)/shard_map/all_to_all | solution.py:285
  177.0 5.8 %collective-permute-done.4 = bf16[2,4,2,16,256]{4,3,2,1,0:T(8,128)(2,1)S(1)} collective-permute-done((bf16[2,4,2,16,256]{4,3,2,1,0:T(8,128)(2,1)S(1)}, bf16[2,4,2,16,256]{4,3,2,1,0:T(8,128)(2,1)S(1)}, u32[]{:S(2)}, u32[]{:S(2)}) %collective-permute-start.4) | collective-permute-done | bytes 131104 | tf_op jit(solution)/shard_map/ppermute | solution.py:293
  184.3 4.5 %all-to-all-start.7 = ((bf16[4,6,4,2,16,256]{5,4,3,2,1,0:T(8,128)(2,1)}), bf16[4,6,4,2,16,256]{5,4,3,2,1,0:T(8,128)(2,1)S(1)}, u32[]{:S(2)}, u32[]{:S(2)}) async-start(bf16[4,6,4,2,16,256]{5,4,3,2,1,0:T(8,128)(2,1)} %broadcast_in_dim.35), calls=%async_computation.7 | async-start | bytes 3145728 | tf_op jit(solution)/shard_map/all_to_all | solution.py:285
  190.7 2.8 collective-permute-done.3.other
  194.4 4.0 %shard_map.130 = (bf16[3,2,8,2,2,16,256]{6,5,4,3,2,1,0:T(8,128)(2,1)}, f32[8,8,256]{2,1,0:T(8,128)}) custom-call(s32[4]{0:T(128)S(1)} %pad_add_fusion.meta, bf16[4,3,8,16,128]{4,3,2,1,0:T(8,128)(2,1)S(1)} %copy-done.7, bf16[4,64,2048]{2,1,0:T(8,128)(2,1)S(1)} %all-to-all-done.5.mine, bf16[4,64,2048]{2,1,0:T(8,128)(2,1)} %collective-permute-done.3.other), custom_call_target="tpu_custom_call" | custom-call | tf_op jit(solution)/shard_map/pallas_call | solution.py:368
  198.4 10.5 %all-to-all-done.7.cot_ref = bf16[4,6,4,2,16,256]{5,4,3,2,1,0:T(8,128)(2,1)S(1)} async-done(((bf16[4,6,4,2,16,256]{5,4,3,2,1,0:T(8,128)(2,1)}), bf16[4,6,4,2,16,256]{5,4,3,2,1,0:T(8,128)(2,1)S(1)}, u32[]{:S(2)}, u32[]{:S(2)}) %all-to-all-start.7) | async-done | bytes 1572896 | tf_op jit(solution)/shard_map/all_to_all | solution.py:285
  208.9 8.0 %all-to-all-start.6 = ((f32[8,8,256]{2,1,0:T(8,128)}), f32[8,8,256]{2,1,0:T(8,128)S(1)}, u32[]{:S(2)}, u32[]{:S(2)}) async-start(f32[8,8,256]{2,1,0:T(8,128)} %get-tuple-element.14), calls=%async_computation.6 | async-start | bytes 131072 | tf_op jit(solution)/shard_map/all_to_all | solution.py:377
  216.9 3.7 %fusion = bf16[8,4,4,2,27,256]{5,0,4,1,2,3:T(8,128)(2,1)S(1)} fusion(bf16[1,4,4,8,27,256]{5,3,4,2,1,0:T(8,128)(2,1)} %bitcast.14, bf16[1,4,4,8,27,256]{5,3,4,2,1,0:T(8,128)(2,1)} %bitcast.13, pred[]{:T(512)S(6)} %eq.3), kind=kLoop, calls=%fused_computation.1 | loop fusion | flops 5308416 | bytes 7077889 | tf_op jit(solution)/shard_map/transpose | solution.py:353
  220.6 2.9 %copy.26 = bf16[8,4,4,2,27,256]{5,4,3,2,1,0:T(8,128)(2,1)} copy(bf16[8,4,4,2,27,256]{5,0,4,1,2,3:T(8,128)(2,1)S(1)} %fusion) | data formatting | bytes 7077888 | tf_op jit(solution)/shard_map/transpose | solution.py:353
  223.6 6.5 %reshape.38.w_ref = bf16[6912,256]{1,0:T(8,128)(2,1)} reshape(bf16[8,4,4,2,27,256]{5,4,3,2,1,0:T(8,128)(2,1)} %copy.26) | data formatting | bytes 7077888 | tf_op jit(solution)/shard_map/reshape | solution.py:353
  231.5 4.1 %shard_map.133.ga_ref = f32[512,256]{1,0:T(8,128)S(1)} custom-call(s32[4]{0:T(128)S(1)} %pad_add_fusion.meta, bf16[4,6,4,2,16,256]{5,4,3,2,1,0:T(8,128)(2,1)S(1)} %copy-done.3, bf16[6912,256]{1,0:T(8,128)(2,1)} %reshape.38.w_ref), custom_call_target="tpu_custom_call" | custom-call | tf_op jit(solution)/shard_map/pallas_call | solution.py:359
  238.5 10.7 %all-to-all-start.11 = ((f32[32,8,256]{2,1,0:T(8,128)}), f32[32,8,256]{2,1,0:T(8,128)S(1)}, u32[]{:S(2)}, u32[]{:S(2)}) async-start(f32[32,8,256]{2,1,0:T(8,128)} %get-tuple-element.16), calls=%async_computation.11 | async-start | bytes 524288 | tf_op jit(solution)/shard_map/all_to_all | solution.py:386
  253.1 6.4 %shard_map.131 = (bf16[8,72,256]{2,1,0:T(8,128)(2,1)S(1)}, bf16[6,18,4,16,256]{4,3,2,1,0:T(8,128)(2,1)}) custom-call(s32[4]{0:T(128)S(1)} %pad_add_fusion.meta, bf16[6,16,2,16,256]{4,3,2,1,0:T(8,128)(2,1)S(1)} %bitcast.25, f32[8,8,256]{2,1,0:T(8,128)S(1)} %all-to-all-done.6.stats_ref, f32[1,256]{1,0:T(1,128)S(1)} %bitcast.30, f32[1,256]{1,0:T(1,128)S(1)} %bitcast.33, ...), custom_call_target="tpu_custom_call" | custom-call | tf_op jit(solution)/shard_map/pallas_call | solution.py:388
  260.2 5.2 %all-to-all-done.11.sums_ref = f32[32,8,256]{2,1,0:T(8,128)S(1)} async-done(((f32[32,8,256]{2,1,0:T(8,128)}), f32[32,8,256]{2,1,0:T(8,128)S(1)}, u32[]{:S(2)}, u32[]{:S(2)}) %all-to-all-start.11) | async-done | bytes 262176 | tf_op jit(solution)/shard_map/all_to_all | solution.py:386
  265.4 5.8 %all-to-all-start.12 = ((bf16[8,72,256]{2,1,0:T(8,128)(2,1)}), bf16[8,72,256]{2,1,0:T(8,128)(2,1)S(1)}, u32[]{:S(2)}, u32[]{:S(2)}) async-start(bf16[8,72,256]{2,1,0:T(8,128)(2,1)} %copy-done.13), calls=%async_computation.12 | async-start | bytes 589824 | tf_op jit(solution)/shard_map/all_to_all | solution.py:396
  271.2 5.9 %shard_map.132 = bf16[4,4,32,256]{3,2,1,0:T(8,128)(2,1)} custom-call(s32[4]{0:T(128)S(1)} %pad_add_fusion.meta, bf16[6,16,2,16,256]{4,3,2,1,0:T(8,128)(2,1)S(1)} %bitcast.26, bf16[6,18,4,16,256]{4,3,2,1,0:T(8,128)(2,1)} %get-tuple-element.15.q_ref, bf16[6912,256]{1,0:T(8,128)(2,1)} %reshape.38.w_ref), custom_call_target="tpu_custom_call" | custom-call | tf_op jit(solution)/shard_map/pallas_call | solution.py:399
  279.4 7.7 %all-to-all-done.12 = bf16[8,72,256]{2,1,0:T(8,128)(2,1)S(1)} async-done(((bf16[8,72,256]{2,1,0:T(8,128)(2,1)}), bf16[8,72,256]{2,1,0:T(8,128)(2,1)S(1)}, u32[]{:S(2)}, u32[]{:S(2)}) %all-to-all-start.12) | async-done | bytes 294944 | tf_op jit(solution)/shard_map/all_to_all | solution.py:396
  (80 shorter events, 40.6 us)
Async XLA Ops:
  0.6 133.2 %copy-start = (bf16[128,2048]{1,0:T(8,128)(2,1)S(1)}, bf16[128,2048]{1,0:T(8,128)(2,1)}, u32[]{:S(2)}) copy-start(bf16[128,2048]{1,0:T(8,128)(2,1)} %param.13) | copy-start | bytes 1572868
  2.1 23.8 %all-to-all-start.8 = ((bf16[8,27,256]{2,1,0:T(8,128)(2,1)}), bf16[8,27,256]{2,1,0:T(8,128)(2,1)S(1)}, u32[]{:S(2)}, u32[]{:S(2)}) async-start(bf16[8,27,256]{2,1,0:T(8,128)(2,1)} %broadcast_in_dim.36), calls=%async_computation.8 | async-start | bytes 262144 | tf_op jit(solution)/shard_map/all_to_all | solution.py:285
  14.8 0.8 copy-start.11
  25.9 20.6 %all-to-all-start.1 = ((f32[32,8,128]{2,1,0:T(8,128)}), f32[32,8,128]{2,1,0:T(8,128)S(1)}, u32[]{:S(2)}, u32[]{:S(2)}) async-start(f32[32,8,128]{2,1,0:T(8,128)} %shard_map.128), calls=%async_computation.1 | async-start | bytes 262144 | tf_op jit(solution)/shard_map/all_to_all | solution.py:327
  33.8 11.2 %collective-permute-start.1 = (bf16[2,8,16,128]{3,2,1,0:T(8,128)(2,1)}, bf16[2,8,16,128]{3,2,1,0:T(8,128)(2,1)S(1)}, u32[]{:S(2)}, u32[]{:S(2)}) collective-permute-start(bf16[2,8,16,128]{3,2,1,0:T(8,128)(2,1)} %x_ref.1), channel_id=1, source_target_pairs={{0,4},{4,8},{8,12},{12,16},{16,20},{20,24},{24,28},{1,5},{5,9},{9,... | collective-permute-start | bytes 196616 | tf_op jit(solution)/shard_map/ppermute | solution.py:293
  37.9 7.1 %collective-permute-start = (bf16[1,8,16,128]{3,2,1,0:T(8,128)(2,1)S(1)}, bf16[1,8,16,128]{3,2,1,0:T(8,128)(2,1)S(1)}, u32[]{:S(2)}, u32[]{:S(2)}) collective-permute-start(bf16[1,8,16,128]{3,2,1,0:T(8,128)(2,1)S(1)} %slice.15), channel_id=1, source_target_pairs={{0,8},{4,12},{8,16},{12,20},{16,24},{20,28},{1,9},{5,13},{9,17},{1... | collective-permute-start | bytes 98312 | tf_op jit(solution)/shard_map/ppermute | solution.py:293
  47.6 12.5 %all-to-all-start = ((bf16[4,5,8,16,128]{4,3,2,1,0:T(8,128)(2,1)}), bf16[4,5,8,16,128]{4,3,2,1,0:T(8,128)(2,1)S(1)}, u32[]{:S(2)}, u32[]{:S(2)}) async-start(bf16[4,5,8,16,128]{4,3,2,1,0:T(8,128)(2,1)} %broadcast_in_dim.26), calls=%async_computation | async-start | bytes 1310720 | tf_op jit(solution)/shard_map/all_to_all | solution.py:285
  60.0 40.1 %copy-start.4 = (bf16[4,5,8,16,128]{4,3,2,1,0:T(8,128)(2,1)}, bf16[4,5,8,16,128]{4,3,2,1,0:T(8,128)(2,1)S(1)}, u32[]{:S(2)}) copy-start(bf16[4,5,8,16,128]{4,3,2,1,0:T(8,128)(2,1)S(1)} %all-to-all-done.lat_ref) | copy-start | bytes 1966084
  60.9 11.1 %all-to-all-start.9 = ((bf16[4,8,27,256]{3,1,2,0:T(8,128)(2,1)}), bf16[4,8,27,256]{3,1,2,0:T(8,128)(2,1)S(1)}, u32[]{:S(2)}, u32[]{:S(2)}) async-start(bf16[4,8,27,256]{3,1,2,0:T(8,128)(2,1)} %broadcast_in_dim.37), calls=%async_computation.9 | async-start | bytes 884736 | tf_op jit(solution)/shard_map/all_to_all | solution.py:285
  72.0 28.2 %copy-start.18 = (bf16[4,8,27,256]{3,1,2,0:T(8,128)(2,1)}, bf16[4,8,27,256]{3,1,2,0:T(8,128)(2,1)S(1)}, u32[]{:S(2)}) copy-start(bf16[4,8,27,256]{3,1,2,0:T(8,128)(2,1)S(1)} %all-to-all-done.9) | copy-start | bytes 1327108
  100.4 25.7 %copy-start.19 = (bf16[4,8,27,256]{3,1,2,0:T(8,128)(2,1)S(1)}, bf16[4,8,27,256]{3,1,2,0:T(8,128)(2,1)}, u32[]{:S(2)}) copy-start(bf16[4,8,27,256]{3,1,2,0:T(8,128)(2,1)} %copy-done.18) | copy-start | bytes 1327108
  127.5 24.3 %all-to-all-start.10 = ((bf16[4,4,8,27,256]{4,2,3,1,0:T(8,128)(2,1)}), bf16[4,4,8,27,256]{4,2,3,1,0:T(8,128)(2,1)}, u32[]{:S(2)}, u32[]{:S(2)}) async-start(bf16[4,4,8,27,256]{4,2,3,1,0:T(8,128)(2,1)} %broadcast_in_dim.38), calls=%async_computation.10 | async-start | bytes 3538944 | tf_op jit(solution)/shard_map/all_to_all | solution.py:285
  131.9 26.5 %collective-permute-start.2 = (bf16[4,8,224,128]{3,2,1,0:T(8,128)(2,1)S(1)}, bf16[4,8,224,128]{3,2,1,0:T(8,128)(2,1)}, u32[]{:S(2)}, u32[]{:S(2)}) collective-permute-start(bf16[4,8,224,128]{3,2,1,0:T(8,128)(2,1)S(1)} %all_to_all.66.mine), channel_id=1, source_target_pairs={{0,32},{32,0},{1,33},{33,1},{2,34},{34,2},{3,35},{35,3},{4,36},{36... | collective-permute-start | bytes 5505032 | tf_op jit(solution)/shard_map/ppermute | solution.py:289
  152.9 14.7 %all-to-all-start.5 = ((bf16[4,64,2048]{2,1,0:T(8,128)(2,1)}), bf16[4,64,2048]{2,1,0:T(8,128)(2,1)S(1)}, u32[]{:S(2)}, u32[]{:S(2)}) async-start(bf16[4,64,2048]{2,1,0:T(8,128)(2,1)} %broadcast_in_dim.32), calls=%async_computation.5 | async-start | bytes 2097152 | tf_op jit(solution)/shard_map/all_to_all | solution.py:285
  156.4 60.5 %collective-permute-start.5 = (bf16[4,4,8,27,256]{4,2,3,1,0:T(8,128)(2,1)}, bf16[4,4,8,27,256]{4,2,3,1,0:T(8,128)(2,1)}, u32[]{:S(2)}, u32[]{:S(2)}) collective-permute-start(bf16[4,4,8,27,256]{4,2,3,1,0:T(8,128)(2,1)} %all-to-all-done.10), channel_id=1, source_target_pairs={{0,32},{32,0},{1,33},{33,1},{2,34},{34,2},{3,35},{35,3},{4,36},{36... | collective-permute-start | bytes 5308424 | tf_op jit(solution)/shard_map/ppermute | solution.py:289
  158.4 1.1 copy-start.5
  169.3 13.6 %all-to-all-start.4 = ((bf16[4,3,8,16,128]{4,3,2,1,0:T(8,128)(2,1)}), bf16[4,3,8,16,128]{4,3,2,1,0:T(8,128)(2,1)S(1)}, u32[]{:S(2)}, u32[]{:S(2)}) async-start(bf16[4,3,8,16,128]{4,3,2,1,0:T(8,128)(2,1)} %broadcast_in_dim.31), calls=%async_computation.4 | async-start | bytes 786432 | tf_op jit(solution)/shard_map/all_to_all | solution.py:285
  175.1 7.7 %collective-permute-start.4 = (bf16[2,4,2,16,256]{4,3,2,1,0:T(8,128)(2,1)S(1)}, bf16[2,4,2,16,256]{4,3,2,1,0:T(8,128)(2,1)S(1)}, u32[]{:S(2)}, u32[]{:S(2)}) collective-permute-start(bf16[2,4,2,16,256]{4,3,2,1,0:T(8,128)(2,1)S(1)} %slice.20), channel_id=1, source_target_pairs={{4,0},{8,4},{12,8},{16,12},{20,16},{24,20},{28,24},{5,1},{9,5},{13... | collective-permute-start | bytes 393224 | tf_op jit(solution)/shard_map/ppermute | solution.py:293
  182.9 1.4 copy-start.6
  184.3 24.6 %all-to-all-start.7 = ((bf16[4,6,4,2,16,256]{5,4,3,2,1,0:T(8,128)(2,1)}), bf16[4,6,4,2,16,256]{5,4,3,2,1,0:T(8,128)(2,1)S(1)}, u32[]{:S(2)}, u32[]{:S(2)}) async-start(bf16[4,6,4,2,16,256]{5,4,3,2,1,0:T(8,128)(2,1)} %broadcast_in_dim.35), calls=%async_computation.7 | async-start | bytes 3145728 | tf_op jit(solution)/shard_map/all_to_all | solution.py:285
  188.7 4.7 %collective-permute-start.3 = (bf16[4,64,2048]{2,1,0:T(8,128)(2,1)S(1)}, bf16[4,64,2048]{2,1,0:T(8,128)(2,1)}, u32[]{:S(2)}, u32[]{:S(2)}) collective-permute-start(bf16[4,64,2048]{2,1,0:T(8,128)(2,1)S(1)} %all-to-all-done.5.mine), channel_id=1, source_target_pairs={{0,32},{32,0},{1,33},{33,1},{2,34},{34,2},{3,35},{35,3},{4,36},{36... | collective-permute-start | bytes 3145736 | tf_op jit(solution)/shard_map/ppermute | solution.py:289
  193.4 1.0 copy-start.7
  208.9 11.8 %copy-start.2 = (bf16[4,6,4,2,16,256]{5,4,3,2,1,0:T(8,128)(2,1)}, bf16[4,6,4,2,16,256]{5,4,3,2,1,0:T(8,128)(2,1)S(1)}, u32[]{:S(2)}) copy-start(bf16[4,6,4,2,16,256]{5,4,3,2,1,0:T(8,128)(2,1)S(1)} %all-to-all-done.7.cot_ref) | copy-start | bytes 4718596
  208.9 26.8 %all-to-all-start.6 = ((f32[8,8,256]{2,1,0:T(8,128)}), f32[8,8,256]{2,1,0:T(8,128)S(1)}, u32[]{:S(2)}, u32[]{:S(2)}) async-start(f32[8,8,256]{2,1,0:T(8,128)} %get-tuple-element.14), calls=%async_computation.6 | async-start | bytes 131072 | tf_op jit(solution)/shard_map/all_to_all | solution.py:377
  230.1 1.4 copy-start.3
  231.5 4.2 %copy-start.1 = (bf16[3,2,8,2,2,16,256]{6,5,4,3,2,1,0:T(8,128)(2,1)S(1)}, bf16[3,2,8,2,2,16,256]{6,5,4,3,2,1,0:T(8,128)(2,1)}, u32[]{:S(2)}) copy-start(bf16[3,2,8,2,2,16,256]{6,5,4,3,2,1,0:T(8,128)(2,1)} %get-tuple-element.13) | copy-start | bytes 4718596
  231.5 4.2 %copy-start.14 = (f32[256]{0:T(256)S(1)}, f32[256]{0:T(256)}, u32[]{:S(2)}) copy-start(f32[256]{0:T(256)} %param.14) | copy-start | bytes 3076
  231.5 4.2 %copy-start.15 = (f32[256]{0:T(256)S(1)}, f32[256]{0:T(256)}, u32[]{:S(2)}) copy-start(f32[256]{0:T(256)} %param.15) | copy-start | bytes 3076
  238.5 26.9 %all-to-all-start.11 = ((f32[32,8,256]{2,1,0:T(8,128)}), f32[32,8,256]{2,1,0:T(8,128)S(1)}, u32[]{:S(2)}, u32[]{:S(2)}) async-start(f32[32,8,256]{2,1,0:T(8,128)} %get-tuple-element.16), calls=%async_computation.11 | async-start | bytes 524288 | tf_op jit(solution)/shard_map/all_to_all | solution.py:386
  265.4 21.8 %all-to-all-start.12 = ((bf16[8,72,256]{2,1,0:T(8,128)(2,1)}), bf16[8,72,256]{2,1,0:T(8,128)(2,1)S(1)}, u32[]{:S(2)}, u32[]{:S(2)}) async-start(bf16[8,72,256]{2,1,0:T(8,128)(2,1)} %copy-done.13), calls=%async_computation.12 | async-start | bytes 589824 | tf_op jit(solution)/shard_map/all_to_all | solution.py:396
  271.2 5.9 %copy-start.8 = (bf16[4,4,32,256]{3,2,1,0:T(8,128)(2,1)S(1)}, bf16[4,4,32,256]{3,2,1,0:T(8,128)(2,1)}, u32[]{:S(2)}) copy-start(bf16[4,4,32,256]{3,2,1,0:T(8,128)(2,1)} %cot_ref.1) | copy-start | bytes 786436
  271.2 5.9 %copy-start.10 = (f32[512,256]{1,0:T(8,128)S(1)}, f32[512,256]{1,0:T(8,128)}, u32[]{:S(2)}) copy-start(f32[512,256]{1,0:T(8,128)} %copy-done.9) | copy-start | bytes 1572868
  (5 other events, 3.5 us)

commit v2 on v1

v2 whole, which is shorter than its diff:
```python
import jax
import jax.numpy as jnp
from jax import lax
from jax.experimental import pallas as pl
from jax.experimental.pallas import tpu as pltpu
from jax.sharding import Mesh, PartitionSpec as P

EPS = 1e-6
BF = jnp.bfloat16
F32 = jnp.float32
VM = pl.BlockSpec(memory_space=pltpu.VMEM)
SM = pl.BlockSpec(memory_space=pltpu.SMEM)
HB = pl.BlockSpec(memory_space=pl.ANY)
PARAMS = pltpu.CompilerParams(vmem_limit_bytes=50 * 1024 * 1024)


def dot(a, b, precision=None):
    return jnp.dot(a, b, preferred_element_type=F32, precision=precision)


def sigmoid(v):
    return 0.5 * jnp.tanh(0.5 * v) + 0.5


def transpose_kernel(cot_ref, out_ref):
    for k in range(4):
        out_ref[k] = cot_ref[k, 0:4].reshape(512, 256).astype(F32).T.astype(BF)


def group_matrix(channels, per_group):
    rows = lax.broadcasted_iota(jnp.int32, (channels, channels), 0) // per_group
    cols = lax.broadcasted_iota(jnp.int32, (channels, channels), 1) // per_group
    return jnp.where(rows == cols, 1.0, 0.0).astype(F32)


def group_sums(sums, per_group):
    return dot(sums, group_matrix(sums.shape[1], per_group), lax.Precision.HIGHEST)


def moved(v, step, cols=16):
    n = v.shape[0]
    col = lax.broadcasted_iota(jnp.int32, v.shape, 0) % cols
    if step < 0:
        return jnp.where(col == 0, 0.0, pltpu.roll(v, 1, 0))
    return jnp.where(col == cols - 1, 0.0, pltpu.roll(v, n - 1, 0))


def three_terms(v):
    terms = []
    for k in range(3):
        term = v.astype(BF).astype(F32)
        v = v - term
        terms.append(term)
    return terms


def latent_sums_kernel(x_ref, out_ref):
    v = x_ref[...].reshape(-1, 128).astype(F32)
    rows = jnp.concatenate(
        [
            jnp.sum(v, axis=0, keepdims=True),
            jnp.sum(v * v, axis=0, keepdims=True),
            jnp.zeros((6, 128), F32),
        ],
        axis=0,
    )
    out_ref[...] = jnp.broadcast_to(rows[None], out_ref.shape)


def latent_pack_kernel(x_ref, one_ref, two_ref, stats_ref, gain_ref, shift_ref, out_ref):
    total = stats_ref[0]
    for k in range(1, 8):
        total = total + stats_ref[k]
    terms = []
    for v in (total[0:1], total[1:2], gain_ref[...], shift_ref[...]):
        terms += three_terms(v)
    terms = jnp.concatenate(terms + [jnp.zeros((4, 128), F32)], axis=0).astype(BF)
    for k in range(4):
        out_ref[k, 0:128] = two_ref[...].reshape(128, 128)
        out_ref[k, 128:384] = one_ref[...].reshape(256, 128)
        out_ref[k, 384:640] = x_ref[...].reshape(256, 128)
        out_ref[k, 640:656] = terms


def shard_slots(t, core):
    two = t - 2 * (1 - 2 * core)
    return [v & 7 for v in (t, t + 4, t + 7, t + 3, t + 1, t + 5, two + 8, two + 12)]


def each_core(core, mine, other, copies):
    @pl.when(core == 0)
    def _():
        copies(mine, other)

    @pl.when(core == 1)
    def _():
        copies(other, mine)


def latent_conv_kernel(
    meta, lat_ref, m0, m1, o0, o1, out_ref, act, w, sem
):
    core, t, h, x = meta[0], meta[1], meta[2], meta[3]

    def weight_copies(low, high):
        copies = []
        for side, sources in enumerate((low, high)):
            slots = shard_slots(t, side)
            for hop, source in enumerate(sources):
                for two in range(2):
                    xi = (x + (hop if side == 1 else 4 - hop) + 2 * two) & 3
                    for k in range(8):
                        at = pl.multiple_of(slots[k] * 1728 + xi * 432 + side * 208, 16)
                        size = 208 if side == 0 else 224
                        copies.append(
                            pltpu.make_async_copy(
                                source.at[two, k, pl.ds(0, size)], w.at[pl.ds(at, size)], sem
                            )
                        )
        return copies

    def start(low, high):
        for c in weight_copies(low, high):
            c.start()

    each_core(core, (m0, m1), (o0, o1), start)

    frame = lax.broadcasted_iota(jnp.int32, (640, 128), 0) // 128
    inside = frame + 2 * t - 3 >= 0
    zero_row = jnp.zeros((5, 1, 16, 128), BF)
    for j in range(4):
        lanes = slice(j * 128, j * 128 + 128)
        terms = lat_ref[j, 640:656].astype(F32)
        first, second, gain, shift = (
            terms[k : k + 1] + terms[k + 1 : k + 2] + terms[k + 2 : k + 3] for k in (0, 3, 6, 9)
        )
        part = jnp.concatenate([first, second, jnp.zeros((6, 128), F32)], axis=0)
        total = group_sums(part, 16) * (1.0 / 32768.0)
        mean = total[0:1]
        inverse = lax.rsqrt(total[1:2] - mean * mean + EPS)
        v = lat_ref[j, 0:640].astype(F32)
        normed = (v - mean) * inverse * gain + shift
        a = jnp.where(inside, normed * sigmoid(normed), 0.0)
        a = a.astype(BF).astype(F32)
        for dc in range(3):
            s = a if dc == 1 else moved(a, dc - 1)
            act[dc, :, 1:9, :, lanes] = s.astype(BF).reshape(5, 8, 16, 128)
            act[dc, :, 0:1, :, lanes] = zero_row
            act[dc, :, 9:10, :, lanes] = zero_row

    def wait(low, high):
        for c in weight_copies(low, high):
            c.wait()

    each_core(core, (m0, m1), (o0, o1), wait)
    acc = lat_ref[h, 256:640].astype(F32)
    total = None
    for lag in range(3):
        for dr in range(3):
            for dc in range(3):
                tap = (lag * 3 + dr) * 3 + dc
                window = act[dc, lag : lag + 3, dr : dr + 8].reshape(384, 512)
                term = dot(window, w[tap * 512 : tap * 512 + 512, :])
                total = term if total is None else total + term
    out_ref[...] = (acc + total).astype(BF).reshape(3, 8, 16, 128)


def upsample_kernel(meta, pair, rest, mine, other, up_ref, sums_ref, w, sem):
    core, h = meta[0], meta[2]
    copies = []
    for j in range(4):
        hop, two = (h - j) & 1, ((h - j) >> 1) & 1
        slot = jnp.where(hop == 0, two, jnp.where(core == 0, 2 + two, 3 - two))
        at = slot * 128
        for side, source in ((core, mine), (1 - core, other)):
            rows = pl.ds(pl.multiple_of(at + side * 64, 64), 64)
            copies.append(pltpu.make_async_copy(source.at[j], w.at[rows], sem))
    for c in copies:
        c.start()
    for c in copies:
        c.wait()
    x = jnp.concatenate([r[k].reshape(384, 128) for r in (pair, rest) for k in range(2)], axis=1)
    first = jnp.zeros((1, 256), F32)
    second = jnp.zeros((1, 256), F32)
    for p in range(2):
        for q in range(2):
            for s in range(2):
                at = ((p * 2 + q) * 2 + s) * 256
                e = dot(x, w[:, at : at + 256]).astype(BF)
                up_ref[:, p, :, q, s] = e.reshape(3, 8, 16, 256)
                own = e[128:].astype(F32)
                first += jnp.sum(own, axis=0, keepdims=True)
                second += jnp.sum(own * own, axis=0, keepdims=True)
    rows = jnp.concatenate([first, second, jnp.zeros((6, 256), F32)], axis=0)
    sums_ref[...] = jnp.broadcast_to(rows[None], sums_ref.shape)


def grad_active_kernel(meta, cot_ref, got_ref, out_ref, w_ref, q, edges, sem):
    h = meta[2]
    copies = []
    for core in range(2):
        lanes = pl.ds(core * 128, 128)
        for hi in range(4):
            base = hi * 216 - 8 * (hi % 2)
            for xi in range(4):
                first, size = (32, 32) if xi == 3 else (0, 64)
                to = base + (192 if xi == 3 else xi * 64)
                if hi % 2 == 0 and xi == 3:
                    size = 16
                if hi % 2 == 1 and xi == 0:
                    first, size, to = 16, 48, base + 16
                copies.append(
                    pltpu.make_async_copy(
                        got_ref.at[xi, core, hi, :, pl.ds(first, size)],
                        w_ref.at[:, pl.ds(to, size), lanes],
                        sem,
                    )
                )
            xi, row = (3, 48) if hi % 2 == 0 else (0, 0)
            copies.append(
                pltpu.make_async_copy(
                    got_ref.at[xi, core, hi, :, pl.ds(row, 16)], edges.at[core, hi], sem
                )
            )
    for c in copies:
        c.start()
    for row in range(6):
        block = jnp.clip(h + (row + 3) // 4 - 1, 0, 3)
        v = cot_ref[block, :, (row + 3) % 4]
        if row == 0:
            v = jnp.where(h > 0, v, jnp.zeros_like(v))
        if row == 5:
            v = jnp.where(h < 3, v, jnp.zeros_like(v))
        s0, s1 = v[:, 0], v[:, 1]
        q[:, row, 1] = s0
        q[:, row, 2] = s1
        q[:, row, 0] = moved(s1.reshape(96, 256).astype(F32), -1).astype(BF).reshape(6, 16, 256)
        q[:, row, 3] = moved(s0.reshape(96, 256).astype(F32), 1).astype(BF).reshape(6, 16, 256)
    for c in copies:
        c.wait()
    for core in range(2):
        for pair in range(2):
            edge = edges[core, 2 * pair] + edges[core, 2 * pair + 1]
            at = pair * 432 + 208
            w_ref[:, at : at + 16, core * 128 : core * 128 + 128] = edge
    total = None
    w_flat = w_ref.reshape(6912, 256)
    for lag in range(3):
        for dr in range(3):
            for dc in range(3):
                tap = (lag * 3 + dr) * 3 + dc
                window = q[2 - lag : 6 - lag, 2 - dr : 6 - dr, 2 - dc : 4 - dc].reshape(512, 256)
                term = lax.dot_general(
                    window,
                    w_flat[tap * 256 : tap * 256 + 256, :],
                    (((1,), (1,)), ((), ())),
                    preferred_element_type=F32,
                )
                total = term if total is None else total + term
    out_ref[...] = total


def block_moments(stats_ref):
    part = stats_ref[0]
    for k in range(1, 8):
        part = part + stats_ref[k]
    total = group_sums(part, 8) * (1.0 / 131072.0)
    mean = total[0:1]
    return mean, lax.rsqrt(total[1:2] - mean * mean + EPS)


def grad_norm_kernel(meta, up_ref, stats_ref, gain_ref, shift_ref, ga_ref, gn_ref, sums_ref):
    h = meta[2]
    mean, inverse = block_moments(stats_ref)
    own = up_ref[2:6, pl.ds(4 * h, 4)].reshape(512, 256).astype(F32)
    standard = (own - mean) * inverse
    normed = standard * gain_ref[...] + shift_ref[...]
    sigma = sigmoid(normed)
    gn = ga_ref[...] * sigma * (1.0 + normed * (1.0 - sigma))
    gn_ref[...] = gn
    rows = jnp.concatenate(
        [
            jnp.sum(gn, axis=0, keepdims=True),
            jnp.sum(gn * standard, axis=0, keepdims=True),
            jnp.zeros((6, 256), F32),
        ],
        axis=0,
    )
    sums_ref[...] = jnp.broadcast_to(rows[None], sums_ref.shape)


def pack_kernel(gw_ref, sums_ref, out_ref):
    total = sums_ref[0] + sums_ref[1] + sums_ref[2] + sums_ref[3]
    terms = [term[0:2] for term in three_terms(total)]
    terms = jnp.concatenate(terms + [jnp.zeros((2, 256), F32)], axis=0)
    for k in range(8):
        out_ref[k] = jnp.concatenate([gw_ref[k].astype(F32), terms], axis=0).astype(BF)


def weight_grad_kernel(
    meta, up_ref, stats_ref, gain_ref, shift_ref, cot_ref, gw_ref, q_ref, full
):
    t, h = meta[1], meta[2]
    mean, inverse = block_moments(stats_ref)
    scale = inverse * gain_ref[...]
    offset = shift_ref[...] - mean * scale
    q_ref[:, 0:1] = jnp.zeros((6, 1, 4, 16, 256), BF)
    q_ref[:, 17:18] = jnp.zeros((6, 1, 4, 16, 256), BF)
    for f in range(6):
        for s in range(2):
            v = up_ref[f, :, s].reshape(256, 256).astype(F32)
            normed = v * scale + offset
            a = normed * sigmoid(normed)
            if f < 2:
                a = jnp.where(t > 0, a, 0.0)
            a = a.astype(BF)
            a32 = a.astype(F32)
            q_ref[f, 1:17, 1 + s] = a.reshape(16, 16, 256)
            side = moved(a32, 1 if s == 0 else -1).astype(BF).reshape(16, 16, 256)
            q_ref[f, 1:17, 3 if s == 0 else 0] = side
    for dr in range(3):
        for dc in range(3):
            g = None
            for k in range(4):
                window = q_ref[2:6, 4 * k + dr : 4 * k + dr + 4, dc : dc + 2].reshape(512, 256)
                term = dot(cot_ref[k], window)
                g = term if g is None else g + term
            at = (dr * 3 + dc) * 256
            full[at : at + 256, :] = g.T
    for k in range(8):
        gw_ref[k] = full[pl.ds(pl.multiple_of(k * 288 + h * 72, 8), 72), :].astype(BF)


def interleave(scratch, v):
    for half in range(2):
        for s in range(2):
            part = v[:, s, :, half * 128 : half * 128 + 128]
            scratch[half, :, pl.ds(s, 16, stride=2), :] = part
    return jnp.concatenate([scratch[0], scratch[1]], axis=-1)


def decode_kernel(meta, up_ref, q_ref, w_ref, out_ref, scratch):
    h = meta[2]
    total = up_ref[2:6, pl.ds(4 * h, 4)].reshape(512, 256).astype(F32)
    conv = None
    for lag in range(3):
        for dr in range(3):
            for dc in range(3):
                tap = (lag * 3 + dr) * 3 + dc
                window = q_ref[lag : lag + 4, pl.ds(4 * h + dr, 4), dc : dc + 2].reshape(512, 256)
                term = dot(window, w_ref[tap * 256 : tap * 256 + 256, :])
                conv = term if conv is None else conv + term
    mixed = interleave(scratch, (total + conv).reshape(16, 2, 16, 256))
    out_ref[...] = mixed.astype(BF).reshape(4, 4, 32, 256)


def final_kernel(
    meta, up_ref, stats_ref, gain_ref, got_ref, gn_ref, cot_ref, out_ref, gw_ref, totals_ref, scratch
):
    h = meta[2]
    mean, inverse = block_moments(stats_ref)
    got = None
    for k in range(8):
        v = got_ref[k].astype(F32)
        rows = v[72:74] + v[74:76] + v[76:78]
        got = v[0:72] if k == 0 else got + v[0:72]
        total = rows if k == 0 else total + rows
    gw_ref[...] = got
    total = jnp.concatenate([total, jnp.zeros((6, 256), F32)], axis=0)
    totals_ref[...] = total
    gain = gain_ref[...]
    means = group_sums(total * gain, 8) * (1.0 / 131072.0)
    own = up_ref[2:6, pl.ds(4 * h, 4)].reshape(512, 256).astype(F32)
    standard = (own - mean) * inverse
    corrected = (gn_ref[...] * gain - means[0:1] - standard * means[1:2]) * inverse
    corrected = interleave(scratch, corrected.reshape(16, 2, 16, 256))
    cot = cot_ref[...].reshape(16, 32, 256).astype(F32)
    out_ref[...] = (cot + corrected).astype(BF).reshape(4, 4, 32, 256)


def gathered(v, axis, n):
    return lax.all_to_all(jnp.broadcast_to(v[None], (n, *v.shape)), axis, 0, 0, tiled=True)


def swapped(v):
    return lax.ppermute(v, "core", [(0, 1), (1, 0)])


def later(v, step):
    return lax.ppermute(v, "tm", [(i, i + step) for i in range(8) if 0 <= i + step < 8])


def along_z(v, d):
    return lax.ppermute(v, ("zh", "tm"), [(i, (i + d) % 16) for i in range(16)])


def along_z_by_core(v, d):
    pairs = []
    for z in range(16):
        for core in range(2):
            to = (z + (d if core == 0 else -d)) % 16
            pairs.append((((z // 8) * 2 + core) * 8 + z % 8, ((to // 8) * 2 + core) * 8 + to % 8))
    return lax.ppermute(v, ("zh", "core", "tm"), pairs)


def ring_step(v, axis, size, d):
    pairs = []
    for i in range(size):
        for core in range(2):
            to = (i + (d if core == 0 else -d)) % size
            if axis == "x":
                pairs.append((i * 2 + core, to * 2 + core))
            else:
                pairs.append((core * size + i, core * size + to))
    return lax.ppermute(v, ("x", "core") if axis == "x" else ("core", axis), pairs)


def after(v, *others):
    return lax.optimization_barrier((v, *others))[0]


def struct(shape, dtype):
    return jax.ShapeDtypeStruct(shape, dtype)


def call(kernel, out_shape, in_specs, scratch=()):
    several = isinstance(out_shape, list)
    return pl.pallas_call(
        kernel,
        out_shape=out_shape,
        in_specs=in_specs,
        out_specs=[VM] * len(out_shape) if several else VM,
        scratch_shapes=list(scratch),
        compiler_params=PARAMS,
    )


def local(
    latent,
    gain_latent,
    shift_latent,
    conv_latent,
    up_weight,
    gain_block,
    shift_block,
    conv_block,
    cotangent,
):
    x, core = lax.axis_index("x"), lax.axis_index("core")
    t, h = lax.axis_index("tm"), lax.axis_index("height")
    meta = jnp.stack([core, t, h, x]).astype(jnp.int32)
    gain2, shift2 = gain_block[None], shift_block[None]

    piece = lax.dynamic_slice(conv_latent, (x * 432 + core * 208, 0), (224, 128))
    half = lax.dynamic_slice(conv_block, (0, core * 128), (216, 128))
    window = jnp.where(h % 2 == 0, jnp.pad(half, ((0, 8), (0, 0))), jnp.pad(half, ((8, 0), (0, 0))))
    block_piece = lax.dynamic_slice(window, (jnp.minimum(x * 64, 160), 0), (64, 128))
    piece = jnp.concatenate([piece, block_piece])

    sums = call(latent_sums_kernel, struct((8, 8, 128), F32), [VM])(latent)
    stats_latent = lax.all_to_all(sums, "tm", 0, 0, tiled=True)
    two_back, one_back = later(latent[1:], 2), later(latent, 1)

    pair_z = jnp.stack([piece, along_z_by_core(piece, 4)])
    pair_z = after(pair_z, stats_latent, two_back, one_back)
    up_z, down_z, two_z = along_z(pair_z, 1), along_z(pair_z, -1), along_z_by_core(pair_z, 2)
    rows = jnp.concatenate([v[:, :224] for v in (pair_z, up_z, down_z, two_z)])

    near, far = two_z[0, 224:], two_z[1, 224:]
    plus_2, plus_6 = jnp.where(core == 0, far, near), jnp.where(core == 0, near, far)
    steps = [
        pair_z[0, 224:], down_z[0, 224:], plus_2, up_z[1, 224:],
        pair_z[1, 224:], down_z[1, 224:], plus_6, up_z[0, 224:],
    ]
    ordered = lax.dynamic_slice(jnp.stack(steps + steps), ((8 - t) % 8, 0, 0), (8, 64, 128))
    block_w = lax.all_gather(ordered, ("x", "core", "height"))
    block_w = block_w.reshape(4, 2, 4, 8, 64, 128)

    pair_x = jnp.stack([rows, ring_step(rows, "x", 4, 2)])
    lat = call(latent_pack_kernel, struct((4, 656, 128), BF), [VM] * 6)(
        latent, one_back, two_back, stats_latent, gain_latent[None], shift_latent[None]
    )
    lat_all = lax.all_to_all(lat, "height", 0, 0, tiled=True)
    pair_x = after(pair_x, lat_all)
    rest_x = ring_step(pair_x, "x", 4, 1)
    other_pair = swapped(pair_x)

    up_piece = lax.dynamic_slice(up_weight, (core * 64, 0), (64, 2048))
    up_w = gathered(after(up_piece, lat_all), "height", 4)
    phased = cotangent.reshape(4, 4, 16, 2, 256).transpose(0, 1, 3, 2, 4)
    phased = after(phased, lat_all)
    six = jnp.concatenate([phased, later(phased[:2], -1)], 0)
    six = after(six, up_w)
    other_rest = swapped(after(rest_x, up_w, six))

    refined = call(
        latent_conv_kernel,
        struct((3, 8, 16, 128), BF),
        [SM, VM] + [HB] * 4,
        [
            pltpu.VMEM((3, 5, 10, 16, 512), BF),
            pltpu.VMEM((13824, 128), BF),
            pltpu.SemaphoreType.DMA,
        ],
    )(meta, lat_all, pair_x, rest_x, other_pair, other_rest)
    pair_y = jnp.stack([refined, ring_step(refined, "height", 4, 2)])
    rest_y = ring_step(pair_y, "height", 4, 1)

    up_w_other = swapped(after(up_w, refined))
    cot_all = gathered(six, "height", 4)
    cot_t = call(transpose_kernel, struct((4, 256, 512), BF), [VM])(cot_all)
    grad_active, weight = call(
        grad_active_kernel,
        [struct((512, 256), F32), struct((8, 864, 256), BF)],
        [SM, VM, HB],
        [
            pltpu.VMEM((6, 6, 4, 16, 256), BF),
            pltpu.VMEM((2, 4, 8, 16, 128), BF),
            pltpu.SemaphoreType.DMA,
        ],
    )(meta, after(cot_all, cot_t), block_w)
    weight = weight.reshape(6912, 256)

    up, up_sums = call(
        upsample_kernel,
        [struct((3, 2, 8, 2, 2, 16, 256), BF), struct((8, 8, 256), F32)],
        [SM, VM, VM, HB, HB],
        [pltpu.VMEM((512, 2048), BF), pltpu.SemaphoreType.DMA],
    )(meta, pair_y, rest_y, up_w, up_w_other)
    up = up.reshape(6, 16, 2, 16, 256)
    stats_block = lax.all_to_all(up_sums, "tm", 0, 0, tiled=True)

    gn, grad_sums = call(
        grad_norm_kernel, [struct((512, 256), F32), struct((4, 8, 256), F32)], [SM] + [VM] * 5
    )(meta, up, stats_block, gain2, shift2, grad_active)
    all_sums = lax.all_to_all(grad_sums, "height", 0, 0, tiled=True)

    gw, q = call(
        weight_grad_kernel,
        [struct((8, 72, 256), BF), struct((6, 18, 4, 16, 256), BF)],
        [SM] + [VM] * 5,
        [pltpu.VMEM((2304, 256), F32)],
    )(meta, up, stats_block, gain2, shift2, cot_t)
    packed = call(pack_kernel, struct((8, 80, 256), BF), [VM] * 2)(gw, all_sums)
    got = lax.all_to_all(packed, "tm", 0, 0, tiled=True)

    decoded = call(
        decode_kernel,
        struct((4, 4, 32, 256), BF),
        [SM] + [VM] * 3,
        [pltpu.VMEM((2, 16, 32, 128), F32)],
    )(meta, up, q, weight)

    grad_up, grad_weight, totals = call(
        final_kernel,
        [struct((4, 4, 32, 256), BF), struct((72, 256), F32), struct((8, 256), F32)],
        [SM] + [VM] * 6,
        [pltpu.VMEM((2, 16, 32, 128), F32)],
    )(meta, up, stats_block, gain2, got, gn, cotangent)
    return decoded, grad_up, grad_weight, totals[1], totals[0]


def solution(mesh):
    fine = Mesh(
        mesh.devices.reshape(4, 2, 2, 8, 4), ("x", "zh", "core", "tm", "height")
    )
    dp = ("x", "zh", "core")
    return jax.shard_map(
        local,
        mesh=fine,
        in_specs=(
            P((*dp, "tm"), None, None, "height"),
            P("height"),
            P("height"),
            P("tm", "height"),
            P("height", None),
            P(),
            P(),
            P(("tm", "height"), None),
            P((*dp, "tm"), "height", None, None),
        ),
        out_specs=(
            P((*dp, "tm"), "height", None, None),
            P((*dp, "tm"), "height", None, None),
            P((*dp, "tm", "height"), None),
            P(dp),
            P(dp),
        ),
        check_vma=False,
    )
```

time: 290 us -> 216 us (0.74)
  the two profiles are of different devices: /device:TPU:32 before, /device:TPU:2 now
where the time goes in v2:
time: 216 us; the launch traced here: 214 us
  starting transfers between devices  87.4 us (40%)
  waiting for transfers between devices  62.4 us (29%)
  Pallas kernels  33.1 us (15%)
  local copies, waits for them, and re-layouts  15.5 us (7%)
  between operations  14.6 us (7%)
    ppermute x4, waiting for transfers between devices, ring_step(): lax.ppermute(v, ('x', 'core') if axis == 'x' else ('core', axis), pairs)  26 us
    ppermute x4, starting transfers between devices, ring_step(): lax.ppermute(v, ('x', 'core') if axis == 'x' else ('core', axis), pairs)  13.6 us
    ppermute x2, starting transfers between devices, along_z_by_core(): return lax.ppermute(v, ('zh', 'core', 'tm'), pairs)  11.4 us
    all_to_all x1, waiting for transfers between devices, local(): got = lax.all_to_all(packed, 'tm', 0, 0, tiled=True)  10.8 us
    ppermute x3, starting transfers between devices, later(): lax.ppermute(v, 'tm', [(i, i + step) for i in range(8) if 0 <= i + step <...  9.89 us
    unnamed x49, local copies, waits for them, and re-layouts  9.09 us
    all_to_all x1, starting transfers between devices, local(): got = lax.all_to_all(packed, 'tm', 0, 0, tiled=True)  8.9 us
    all_to_all x1, starting transfers between devices, local(): stats_latent = lax.all_to_all(sums, 'tm', 0, 0, tiled=True)  8.48 us
  transfers between devices with their start and end apart: 22, of which 13 were waited for; matrix products, arithmetic and copies ran while one was open for 2% of the time, Pallas kernels for 13%

profile of v2, /device:TPU:2, one launch (start us, length us, event | category | flops | bytes accessed | tf_op | source)
XLA Modules:
  0.0 214.4 jit_solution(7408730033058258515)
XLA Ops:
  9.0 9.1 %collective-permute-start.2 = (bf16[288,128]{1,0:T(8,128)(2,1)S(1)}, bf16[288,128]{1,0:T(8,128)(2,1)S(1)}, u32[]{:S(2)}, u32[]{:S(2)}) collective-permute-start(bf16[288,128]{1,0:T(8,128)(2,1)S(1)} %get-tuple-element.46), channel_id=1, source_target_pairs={{0,16},{32,112},{4,20},{36,116},{8,24},{40,120},{12,28},{44,124},{... | collective-permute-start | bytes 221192 | tf_op jit(solution)/shard_map/ppermute | solution.py:403
  18.1 3.8 %collective-permute-start = (bf16[2,8,16,128]{3,2,1,0:T(8,128)(2,1)}, bf16[2,8,16,128]{3,2,1,0:T(8,128)(2,1)S(1)}, u32[]{:S(2)}, u32[]{:S(2)}) collective-permute-start(bf16[2,8,16,128]{3,2,1,0:T(8,128)(2,1)} %x_ref.3), channel_id=1, source_target_pairs={{0,4},{4,8},{8,12},{12,16},{16,20},{20,24},{24,28},{1,5},{5,9},{9,... | collective-permute-start | bytes 196616 | tf_op jit(solution)/shard_map/ppermute | solution.py:390
  23.4 8.5 %all-to-all-start = ((f32[8,8,128]{2,1,0:T(8,128)}), f32[8,8,128]{2,1,0:T(8,128)S(1)}, u32[]{:S(2)}, u32[]{:S(2)}) async-start(f32[8,8,128]{2,1,0:T(8,128)} %shard_map.128), calls=%async_computation | async-start | bytes 65536 | tf_op jit(solution)/shard_map/all_to_all | solution.py:461
  32.7 4.8 %collective-permute-start.1 = (bf16[1,8,16,128]{3,2,1,0:T(8,128)(2,1)S(1)}, bf16[1,8,16,128]{3,2,1,0:T(8,128)(2,1)S(1)}, u32[]{:S(2)}, u32[]{:S(2)}) collective-permute-start(bf16[1,8,16,128]{3,2,1,0:T(8,128)(2,1)S(1)} %slice.48), channel_id=1, source_target_pairs={{0,8},{4,12},{8,16},{12,20},{16,24},{20,28},{1,9},{5,13},{9,17},{1... | collective-permute-start | bytes 98312 | tf_op jit(solution)/shard_map/ppermute | solution.py:390
  39.1 3.5 %all-to-all-done.stats_ref = f32[8,8,128]{2,1,0:T(8,128)S(1)} async-done(((f32[8,8,128]{2,1,0:T(8,128)}), f32[8,8,128]{2,1,0:T(8,128)S(1)}, u32[]{:S(2)}, u32[]{:S(2)}) %all-to-all-start) | async-done | bytes 32800 | tf_op jit(solution)/shard_map/all_to_all | solution.py:461
  42.6 2.3 %collective-permute-start.5 = (bf16[2,288,128]{2,1,0:T(8,128)(2,1)S(1)}, bf16[2,288,128]{2,1,0:T(8,128)(2,1)S(1)}, u32[]{:S(2)}, u32[]{:S(2)}) collective-permute-start(bf16[2,288,128]{2,1,0:T(8,128)(2,1)S(1)} %pad_maximum_fusion.4), channel_id=1, source_target_pairs={{0,8},{32,120},{4,12},{36,124},{8,16},{40,32},{12,20},{44,36},{16,... | collective-permute-start | bytes 442376 | tf_op jit(solution)/shard_map/ppermute | solution.py:403
  44.9 4.7 %collective-permute-start.4 = (bf16[2,288,128]{2,1,0:T(8,128)(2,1)S(1)}, bf16[2,288,128]{2,1,0:T(8,128)(2,1)S(1)}, u32[]{:S(2)}, u32[]{:S(2)}) collective-permute-start(bf16[2,288,128]{2,1,0:T(8,128)(2,1)S(1)} %pad_maximum_fusion.4), channel_id=1, source_target_pairs={{0,92},{4,0},{8,4},{12,8},{16,12},{20,16},{24,20},{28,24},{64,28},... | collective-permute-start | bytes 442376 | tf_op jit(solution)/shard_map/ppermute | solution.py:394
  49.5 1.9 collective-permute-start.3
  53.3 4.5 %collective-permute-done.3 = bf16[2,288,128]{2,1,0:T(8,128)(2,1)S(1)} collective-permute-done((bf16[2,288,128]{2,1,0:T(8,128)(2,1)S(1)}, bf16[2,288,128]{2,1,0:T(8,128)(2,1)S(1)}, u32[]{:S(2)}, u32[]{:S(2)}) %collective-permute-start.3) | collective-permute-done | bytes 147488 | tf_op jit(solution)/shard_map/ppermute | solution.py:394
  58.8 4.0 %collective-permute-start.6 = (bf16[8,224,128]{2,1,0:T(8,128)(2,1)S(1)}, bf16[8,224,128]{2,1,0:T(8,128)(2,1)S(1)}, u32[]{:S(2)}, u32[]{:S(2)}) collective-permute-start(bf16[8,224,128]{2,1,0:T(8,128)(2,1)S(1)} %get-tuple-element.44), channel_id=1, source_target_pairs={{0,256},{32,288},{128,384},{160,416},{256,0},{288,32},{384,128},{4... | collective-permute-start | bytes 1376264 | tf_op jit(solution)/shard_map/ppermute | solution.py:415
  63.8 4.6 %all-to-all-start.1 = ((bf16[4,656,128]{2,1,0:T(8,128)(2,1)}), bf16[4,656,128]{2,1,0:T(8,128)(2,1)S(1)}, u32[]{:S(2)}, u32[]{:S(2)}) async-start(bf16[4,656,128]{2,1,0:T(8,128)(2,1)} %shard_map.129), calls=%async_computation.1 | async-start | bytes 1343488 | tf_op jit(solution)/shard_map/all_to_all | solution.py:483
  68.4 4.4 %collective-permute-done.6 = bf16[8,224,128]{2,1,0:T(8,128)(2,1)S(1)} collective-permute-done((bf16[8,224,128]{2,1,0:T(8,128)(2,1)S(1)}, bf16[8,224,128]{2,1,0:T(8,128)(2,1)S(1)}, u32[]{:S(2)}, u32[]{:S(2)}) %collective-permute-start.6) | collective-permute-done | bytes 458784 | tf_op jit(solution)/shard_map/ppermute | solution.py:415
  73.8 4.4 %all-to-all-done.1.lat_ref = bf16[4,656,128]{2,1,0:T(8,128)(2,1)S(1)} async-done(((bf16[4,656,128]{2,1,0:T(8,128)(2,1)}), bf16[4,656,128]{2,1,0:T(8,128)(2,1)S(1)}, u32[]{:S(2)}, u32[]{:S(2)}) %all-to-all-start.1) | async-done | bytes 671776 | tf_op jit(solution)/shard_map/all_to_all | solution.py:483
  81.4 3.5 %all-to-all-start.2 = ((bf16[4,64,2048]{2,1,0:T(8,128)(2,1)}), bf16[4,64,2048]{2,1,0:T(8,128)(2,1)S(1)}, u32[]{:S(2)}, u32[]{:S(2)}) async-start(bf16[4,64,2048]{2,1,0:T(8,128)(2,1)} %broadcast_in_dim.26), calls=%async_computation.2 | async-start | bytes 2097152 | tf_op jit(solution)/shard_map/all_to_all | solution.py:382
  86.4 1.9 collective-permute-start.8
  88.3 3.6 %collective-permute-done.9 = bf16[2,4,2,16,256]{4,3,2,1,0:T(8,128)(2,1)S(1)} collective-permute-done((bf16[2,4,2,16,256]{4,3,2,1,0:T(8,128)(2,1)S(1)}, bf16[2,4,2,16,256]{4,3,2,1,0:T(8,128)(2,1)S(1)}, u32[]{:S(2)}, u32[]{:S(2)}) %collective-permute-start.9) | collective-permute-done | bytes 131104 | tf_op jit(solution)/shard_map/ppermute | solution.py:390
  92.0 5.3 %all-to-all-done.2.mine = bf16[4,64,2048]{2,1,0:T(8,128)(2,1)S(1)} async-done(((bf16[4,64,2048]{2,1,0:T(8,128)(2,1)}), bf16[4,64,2048]{2,1,0:T(8,128)(2,1)S(1)}, u32[]{:S(2)}, u32[]{:S(2)}) %all-to-all-start.2) | async-done | bytes 1048608 | tf_op jit(solution)/shard_map/all_to_all | solution.py:382
  100.6 3.7 %all-to-all-start.4 = ((bf16[4,6,4,2,16,256]{5,4,3,2,1,0:T(8,128)(2,1)}), bf16[4,6,4,2,16,256]{5,4,3,2,1,0:T(8,128)(2,1)S(1)}, u32[]{:S(2)}, u32[]{:S(2)}) async-start(bf16[4,6,4,2,16,256]{5,4,3,2,1,0:T(8,128)(2,1)} %broadcast_in_dim.29), calls=%async_computation.4 | async-start | bytes 3145728 | tf_op jit(solution)/shard_map/all_to_all | solution.py:382
  105.4 5.5 %shard_map.130 = bf16[3,8,16,128]{3,2,1,0:T(8,128)(2,1)S(1)} custom-call(s32[4]{0:T(128)S(1)} %pad_add_fusion.meta, bf16[4,656,128]{2,1,0:T(8,128)(2,1)S(1)} %copy-done.5, bf16[2,8,224,128]{3,2,1,0:T(8,128)(2,1)} %pad_maximum_fusion.m0, bf16[2,8,224,128]{3,2,1,0:T(8,128)(2,1)} %collective-permute-done.7.m1, ...), custom_call_target="tpu_custom_call" | custom-call | tf_op jit(solution)/shard_map/pallas_call | solution.py:496
  110.9 2.4 %collective-permute-start.13 = (bf16[4,64,2048]{2,1,0:T(8,128)(2,1)S(1)}, bf16[4,64,2048]{2,1,0:T(8,128)(2,1)S(1)}, u32[]{:S(2)}, u32[]{:S(2)}) collective-permute-start(bf16[4,64,2048]{2,1,0:T(8,128)(2,1)S(1)} %all-to-all-done.2.mine), channel_id=1, source_target_pairs={{0,32},{32,0},{1,33},{33,1},{2,34},{34,2},{3,35},{35,3},{4,36},{36... | collective-permute-start | bytes 3145736 | tf_op jit(solution)/shard_map/ppermute | solution.py:386
  113.4 5.2 %collective-permute-start.11 = (bf16[3,8,16,128]{3,2,1,0:T(8,128)(2,1)S(1)}, bf16[3,8,16,128]{3,2,1,0:T(8,128)(2,1)S(1)}, u32[]{:S(2)}, u32[]{:S(2)}) collective-permute-start(bf16[3,8,16,128]{3,2,1,0:T(8,128)(2,1)S(1)} %shard_map.130), channel_id=1, source_target_pairs={{0,2},{32,34},{1,3},{33,35},{2,0},{34,32},{3,1},{35,33},{4,6},{36,... | collective-permute-start | bytes 294920 | tf_op jit(solution)/shard_map/ppermute | solution.py:415
  118.6 15.3 %collective-permute-done.11 = bf16[3,8,16,128]{3,2,1,0:T(8,128)(2,1)S(1)} collective-permute-done((bf16[3,8,16,128]{3,2,1,0:T(8,128)(2,1)S(1)}, bf16[3,8,16,128]{3,2,1,0:T(8,128)(2,1)S(1)}, u32[]{:S(2)}, u32[]{:S(2)}) %collective-permute-start.11) | collective-permute-done | bytes 98336 | tf_op jit(solution)/shard_map/ppermute | solution.py:415
  133.9 2.5 %collective-permute-start.12 = (bf16[2,3,8,16,128]{4,3,2,1,0:T(8,128)(2,1)S(1)}, bf16[2,3,8,16,128]{4,3,2,1,0:T(8,128)(2,1)S(1)}, u32[]{:S(2)}, u32[]{:S(2)}) collective-permute-start(bf16[2,3,8,16,128]{4,3,2,1,0:T(8,128)(2,1)S(1)} %pad_maximum_fusion.3.pair), channel_id=1, source_target_pairs={{0,1},{32,35},{1,2},{33,32},{2,3},{34,33},{3,0},{35,34},{4,5},{36,... | collective-permute-start | bytes 589832 | tf_op jit(solution)/shard_map/ppermute | solution.py:415
  136.4 6.3 %collective-permute-done.12.rest = bf16[2,3,8,16,128]{4,3,2,1,0:T(8,128)(2,1)S(1)} collective-permute-done((bf16[2,3,8,16,128]{4,3,2,1,0:T(8,128)(2,1)S(1)}, bf16[2,3,8,16,128]{4,3,2,1,0:T(8,128)(2,1)S(1)}, u32[]{:S(2)}, u32[]{:S(2)}) %collective-permute-start.12) | collective-permute-done | bytes 196640 | tf_op jit(solution)/shard_map/ppermute | solution.py:415
  142.7 3.0 %shard_map.131 = (bf16[3,2,8,2,2,16,256]{6,5,4,3,2,1,0:T(8,128)(2,1)}, f32[8,8,256]{2,1,0:T(8,128)}) custom-call(s32[4]{0:T(128)S(1)} %pad_add_fusion.meta, bf16[2,3,8,16,128]{4,3,2,1,0:T(8,128)(2,1)S(1)} %pad_maximum_fusion.3.pair, bf16[2,3,8,16,128]{4,3,2,1,0:T(8,128)(2,1)S(1)} %collective-permute-done.12.rest, ...), custom_call_target="tpu_custom_call" | custom-call | tf_op jit(solution)/shard_map/pallas_call | solution.py:524
  145.7 7.0 %all-to-all-start.3 = ((f32[8,8,256]{2,1,0:T(8,128)}), f32[8,8,256]{2,1,0:T(8,128)S(1)}, u32[]{:S(2)}, u32[]{:S(2)}) async-start(f32[8,8,256]{2,1,0:T(8,128)} %get-tuple-element.32), calls=%async_computation.3 | async-start | bytes 131072 | tf_op jit(solution)/shard_map/all_to_all | solution.py:531
  155.8 6.0 %shard_map.134 = (f32[512,256]{1,0:T(8,128)S(1)}, bf16[8,864,256]{2,1,0:T(8,128)(2,1)}) custom-call(s32[4]{0:T(128)S(1)} %pad_add_fusion.meta, bf16[4,6,4,2,16,256]{5,4,3,2,1,0:T(8,128)(2,1)S(1)} %copy-done.3, bf16[4,2,4,8,64,128]{5,4,3,2,1,0:T(8,128)(2,1)} %bitcast.38), custom_call_target="tpu_custom_call" | custom-call | tf_op jit(solution)/shard_map/pallas_call | solution.py:512
  167.3 3.4 %all-to-all-start.5 = ((f32[4,8,256]{2,1,0:T(8,128)}), f32[4,8,256]{2,1,0:T(8,128)S(1)}, u32[]{:S(2)}, u32[]{:S(2)}) async-start(f32[4,8,256]{2,1,0:T(8,128)} %get-tuple-element.38), calls=%async_computation.5 | async-start | bytes 65536 | tf_op jit(solution)/shard_map/all_to_all | solution.py:536
  170.8 6.4 %shard_map.133 = (bf16[8,72,256]{2,1,0:T(8,128)(2,1)S(1)}, bf16[6,18,4,16,256]{4,3,2,1,0:T(8,128)(2,1)}) custom-call(s32[4]{0:T(128)S(1)} %pad_add_fusion.meta, bf16[6,16,2,16,256]{4,3,2,1,0:T(8,128)(2,1)S(1)} %bitcast.27, f32[8,8,256]{2,1,0:T(8,128)S(1)} %all-to-all-done.3.stats_ref, f32[1,256]{1,0:T(1,128)S(1)} %bitcast.32, f32[1,256]{1,0:T(1,128)S(1)} %bitcast.35, ...), custom_call_target="tpu_custom_call" | custom-call | tf_op jit(solution)/shard_map/pallas_call | solution.py:538
  179.6 8.9 %all-to-all-start.6 = ((bf16[8,80,256]{2,1,0:T(8,128)(2,1)}), bf16[8,80,256]{2,1,0:T(8,128)(2,1)S(1)}, u32[]{:S(2)}, u32[]{:S(2)}) async-start(bf16[8,80,256]{2,1,0:T(8,128)(2,1)} %shard_map.137), calls=%async_computation.6 | async-start | bytes 655360 | tf_op jit(solution)/shard_map/all_to_all | solution.py:545
  188.5 5.9 %shard_map.135 = bf16[4,4,32,256]{3,2,1,0:T(8,128)(2,1)} custom-call(s32[4]{0:T(128)S(1)} %pad_add_fusion.meta, bf16[6,16,2,16,256]{4,3,2,1,0:T(8,128)(2,1)S(1)} %bitcast.28, bf16[6,18,4,16,256]{4,3,2,1,0:T(8,128)(2,1)} %get-tuple-element.33.q_ref, bf16[6912,256]{1,0:T(8,128)(2,1)} %bitcast.39), custom_call_target="tpu_custom_call" | custom-call | tf_op jit(solution)/shard_map/pallas_call | solution.py:547
  194.3 10.8 %all-to-all-done.6.got_ref = bf16[8,80,256]{2,1,0:T(8,128)(2,1)S(1)} async-done(((bf16[8,80,256]{2,1,0:T(8,128)(2,1)}), bf16[8,80,256]{2,1,0:T(8,128)(2,1)S(1)}, u32[]{:S(2)}, u32[]{:S(2)}) %all-to-all-start.6) | async-done | bytes 327712 | tf_op jit(solution)/shard_map/all_to_all | solution.py:545
  (101 shorter events, 32.9 us)
Async XLA Ops:
  7.2 73.0 %copy-start = (bf16[128,2048]{1,0:T(8,128)(2,1)S(1)}, bf16[128,2048]{1,0:T(8,128)(2,1)}, u32[]{:S(2)}) copy-start(bf16[128,2048]{1,0:T(8,128)(2,1)} %param.13) | copy-start | bytes 1572868
  7.2 55.7 %copy-start.12 = (bf16[2,8,16,128]{3,2,1,0:T(8,128)(2,1)S(1)}, bf16[2,8,16,128]{3,2,1,0:T(8,128)(2,1)}, u32[]{:S(2)}) copy-start(bf16[2,8,16,128]{3,2,1,0:T(8,128)(2,1)} %x_ref.3) | copy-start | bytes 196612
  7.2 55.7 %copy-start.18 = (f32[128]{0:T(128)S(1)}, f32[128]{0:T(128)}, u32[]{:S(2)}) copy-start(f32[128]{0:T(128)} %param.11) | copy-start | bytes 1540
  7.2 55.7 %copy-start.17 = (f32[128]{0:T(128)S(1)}, f32[128]{0:T(128)}, u32[]{:S(2)}) copy-start(f32[128]{0:T(128)} %param.10) | copy-start | bytes 1540
  9.0 28.5 %collective-permute-start.2 = (bf16[288,128]{1,0:T(8,128)(2,1)S(1)}, bf16[288,128]{1,0:T(8,128)(2,1)S(1)}, u32[]{:S(2)}, u32[]{:S(2)}) collective-permute-start(bf16[288,128]{1,0:T(8,128)(2,1)S(1)} %get-tuple-element.46), channel_id=1, source_target_pairs={{0,16},{32,112},{4,20},{36,116},{8,24},{40,120},{12,28},{44,124},{... | collective-permute-start | bytes 221192 | tf_op jit(solution)/shard_map/ppermute | solution.py:403
  18.1 21.0 %collective-permute-start = (bf16[2,8,16,128]{3,2,1,0:T(8,128)(2,1)}, bf16[2,8,16,128]{3,2,1,0:T(8,128)(2,1)S(1)}, u32[]{:S(2)}, u32[]{:S(2)}) collective-permute-start(bf16[2,8,16,128]{3,2,1,0:T(8,128)(2,1)} %x_ref.3), channel_id=1, source_target_pairs={{0,4},{4,8},{8,12},{12,16},{16,20},{20,24},{24,28},{1,5},{5,9},{9,... | collective-permute-start | bytes 196616 | tf_op jit(solution)/shard_map/ppermute | solution.py:390
  23.4 19.1 %all-to-all-start = ((f32[8,8,128]{2,1,0:T(8,128)}), f32[8,8,128]{2,1,0:T(8,128)S(1)}, u32[]{:S(2)}, u32[]{:S(2)}) async-start(f32[8,8,128]{2,1,0:T(8,128)} %shard_map.128), calls=%async_computation | async-start | bytes 65536 | tf_op jit(solution)/shard_map/all_to_all | solution.py:461
  31.9 122.3 %all-gather.3.cloned.1.call-start = ((), (), s32[]{:S(2)}) async-start(), calls=%async_computation.7 | async-start | bytes 4325376 | tf_op jit(solution)/shard_map/all_gather | solution.py:476
  32.7 6.4 %collective-permute-start.1 = (bf16[1,8,16,128]{3,2,1,0:T(8,128)(2,1)S(1)}, bf16[1,8,16,128]{3,2,1,0:T(8,128)(2,1)S(1)}, u32[]{:S(2)}, u32[]{:S(2)}) collective-permute-start(bf16[1,8,16,128]{3,2,1,0:T(8,128)(2,1)S(1)} %slice.48), channel_id=1, source_target_pairs={{0,8},{4,12},{8,16},{12,20},{16,24},{20,28},{1,9},{5,13},{9,17},{1... | collective-permute-start | bytes 98312 | tf_op jit(solution)/shard_map/ppermute | solution.py:390
  42.6 10.7 %collective-permute-start.5 = (bf16[2,288,128]{2,1,0:T(8,128)(2,1)S(1)}, bf16[2,288,128]{2,1,0:T(8,128)(2,1)S(1)}, u32[]{:S(2)}, u32[]{:S(2)}) collective-permute-start(bf16[2,288,128]{2,1,0:T(8,128)(2,1)S(1)} %pad_maximum_fusion.4), channel_id=1, source_target_pairs={{0,8},{32,120},{4,12},{36,124},{8,16},{40,32},{12,20},{44,36},{16,... | collective-permute-start | bytes 442376 | tf_op jit(solution)/shard_map/ppermute | solution.py:403
  44.9 8.2 %collective-permute-start.4 = (bf16[2,288,128]{2,1,0:T(8,128)(2,1)S(1)}, bf16[2,288,128]{2,1,0:T(8,128)(2,1)S(1)}, u32[]{:S(2)}, u32[]{:S(2)}) collective-permute-start(bf16[2,288,128]{2,1,0:T(8,128)(2,1)S(1)} %pad_maximum_fusion.4), channel_id=1, source_target_pairs={{0,92},{4,0},{8,4},{12,8},{16,12},{20,16},{24,20},{28,24},{64,28},... | collective-permute-start | bytes 442376 | tf_op jit(solution)/shard_map/ppermute | solution.py:394
  49.5 8.2 %collective-permute-start.3 = (bf16[2,288,128]{2,1,0:T(8,128)(2,1)S(1)}, bf16[2,288,128]{2,1,0:T(8,128)(2,1)S(1)}, u32[]{:S(2)}, u32[]{:S(2)}) collective-permute-start(bf16[2,288,128]{2,1,0:T(8,128)(2,1)S(1)} %pad_maximum_fusion.4), channel_id=1, source_target_pairs={{0,4},{4,8},{8,12},{12,16},{16,20},{20,24},{24,28},{28,64},{64,68}... | collective-permute-start | bytes 442376 | tf_op jit(solution)/shard_map/ppermute | solution.py:394
  58.8 14.0 %collective-permute-start.6 = (bf16[8,224,128]{2,1,0:T(8,128)(2,1)S(1)}, bf16[8,224,128]{2,1,0:T(8,128)(2,1)S(1)}, u32[]{:S(2)}, u32[]{:S(2)}) collective-permute-start(bf16[8,224,128]{2,1,0:T(8,128)(2,1)S(1)} %get-tuple-element.44), channel_id=1, source_target_pairs={{0,256},{32,288},{128,384},{160,416},{256,0},{288,32},{384,128},{4... | collective-permute-start | bytes 1376264 | tf_op jit(solution)/shard_map/ppermute | solution.py:415
  63.8 21.0 %copy-start.6 = (bf16[4,4,32,256]{3,2,1,0:T(8,128)(2,1)S(1)}, bf16[4,4,32,256]{3,2,1,0:T(8,128)(2,1)}, u32[]{:S(2)}) copy-start(bf16[4,4,32,256]{3,2,1,0:T(8,128)(2,1)} %cot_ref.1) | copy-start | bytes 786436
  63.8 14.4 %all-to-all-start.1 = ((bf16[4,656,128]{2,1,0:T(8,128)(2,1)}), bf16[4,656,128]{2,1,0:T(8,128)(2,1)S(1)}, u32[]{:S(2)}, u32[]{:S(2)}) async-start(bf16[4,656,128]{2,1,0:T(8,128)(2,1)} %shard_map.129), calls=%async_computation.1 | async-start | bytes 1343488 | tf_op jit(solution)/shard_map/all_to_all | solution.py:483
  78.3 22.3 %copy-start.4 = (bf16[4,656,128]{2,1,0:T(8,128)(2,1)}, bf16[4,656,128]{2,1,0:T(8,128)(2,1)S(1)}, u32[]{:S(2)}) copy-start(bf16[4,656,128]{2,1,0:T(8,128)(2,1)S(1)} %all-to-all-done.1.lat_ref) | copy-start | bytes 2015236
  78.3 19.0 %collective-permute-start.7 = (bf16[2,8,224,128]{3,2,1,0:T(8,128)(2,1)}, bf16[2,8,224,128]{3,2,1,0:T(8,128)(2,1)}, u32[]{:S(2)}, u32[]{:S(2)}) collective-permute-start(bf16[2,8,224,128]{3,2,1,0:T(8,128)(2,1)} %pad_maximum_fusion.m0), channel_id=1, source_target_pairs={{0,128},{32,416},{128,256},{160,32},{256,384},{288,160},{384,0},{4... | collective-permute-start | bytes 2752520 | tf_op jit(solution)/shard_map/ppermute | solution.py:415
  81.4 15.9 %all-to-all-start.2 = ((bf16[4,64,2048]{2,1,0:T(8,128)(2,1)}), bf16[4,64,2048]{2,1,0:T(8,128)(2,1)S(1)}, u32[]{:S(2)}, u32[]{:S(2)}) async-start(bf16[4,64,2048]{2,1,0:T(8,128)(2,1)} %broadcast_in_dim.26), calls=%async_computation.2 | async-start | bytes 2097152 | tf_op jit(solution)/shard_map/all_to_all | solution.py:382
  85.1 6.9 %collective-permute-start.9 = (bf16[2,4,2,16,256]{4,3,2,1,0:T(8,128)(2,1)S(1)}, bf16[2,4,2,16,256]{4,3,2,1,0:T(8,128)(2,1)S(1)}, u32[]{:S(2)}, u32[]{:S(2)}) collective-permute-start(bf16[2,4,2,16,256]{4,3,2,1,0:T(8,128)(2,1)S(1)} %slice.53), channel_id=1, source_target_pairs={{4,0},{8,4},{12,8},{16,12},{20,16},{24,20},{28,24},{5,1},{9,5},{13... | collective-permute-start | bytes 393224 | tf_op jit(solution)/shard_map/ppermute | solution.py:390
  86.4 18.0 %collective-permute-start.8 = (bf16[2,8,224,128]{3,2,1,0:T(8,128)(2,1)}, bf16[2,8,224,128]{3,2,1,0:T(8,128)(2,1)}, u32[]{:S(2)}, u32[]{:S(2)}) collective-permute-start(bf16[2,8,224,128]{3,2,1,0:T(8,128)(2,1)} %pad_maximum_fusion.m0), channel_id=1, source_target_pairs={{0,32},{32,0},{1,33},{33,1},{2,34},{34,2},{3,35},{35,3},{4,36},{36... | collective-permute-start | bytes 2752520 | tf_op jit(solution)/shard_map/ppermute | solution.py:386
  97.3 7.1 %collective-permute-start.10 = (bf16[2,8,224,128]{3,2,1,0:T(8,128)(2,1)}, bf16[2,8,224,128]{3,2,1,0:T(8,128)(2,1)}, u32[]{:S(2)}, u32[]{:S(2)}) collective-permute-start(bf16[2,8,224,128]{3,2,1,0:T(8,128)(2,1)} %collective-permute-done.7.m1), channel_id=1, source_target_pairs={{0,32},{32,0},{1,33},{33,1},{2,34},{34,2},{3,35},{35,3},{4,36},{36... | collective-permute-start | bytes 2752520 | tf_op jit(solution)/shard_map/ppermute | solution.py:386
  100.6 45.1 %all-to-all-start.4 = ((bf16[4,6,4,2,16,256]{5,4,3,2,1,0:T(8,128)(2,1)}), bf16[4,6,4,2,16,256]{5,4,3,2,1,0:T(8,128)(2,1)S(1)}, u32[]{:S(2)}, u32[]{:S(2)}) async-start(bf16[4,6,4,2,16,256]{5,4,3,2,1,0:T(8,128)(2,1)} %broadcast_in_dim.29), calls=%async_computation.4 | async-start | bytes 3145728 | tf_op jit(solution)/shard_map/all_to_all | solution.py:382
  110.9 31.7 %collective-permute-start.13 = (bf16[4,64,2048]{2,1,0:T(8,128)(2,1)S(1)}, bf16[4,64,2048]{2,1,0:T(8,128)(2,1)S(1)}, u32[]{:S(2)}, u32[]{:S(2)}) collective-permute-start(bf16[4,64,2048]{2,1,0:T(8,128)(2,1)S(1)} %all-to-all-done.2.mine), channel_id=1, source_target_pairs={{0,32},{32,0},{1,33},{33,1},{2,34},{34,2},{3,35},{35,3},{4,36},{36... | collective-permute-start | bytes 3145736 | tf_op jit(solution)/shard_map/ppermute | solution.py:386
  113.4 20.5 %collective-permute-start.11 = (bf16[3,8,16,128]{3,2,1,0:T(8,128)(2,1)S(1)}, bf16[3,8,16,128]{3,2,1,0:T(8,128)(2,1)S(1)}, u32[]{:S(2)}, u32[]{:S(2)}) collective-permute-start(bf16[3,8,16,128]{3,2,1,0:T(8,128)(2,1)S(1)} %shard_map.130), channel_id=1, source_target_pairs={{0,2},{32,34},{1,3},{33,35},{2,0},{34,32},{3,1},{35,33},{4,6},{36,... | collective-permute-start | bytes 294920 | tf_op jit(solution)/shard_map/ppermute | solution.py:415
  133.9 8.8 %collective-permute-start.12 = (bf16[2,3,8,16,128]{4,3,2,1,0:T(8,128)(2,1)S(1)}, bf16[2,3,8,16,128]{4,3,2,1,0:T(8,128)(2,1)S(1)}, u32[]{:S(2)}, u32[]{:S(2)}) collective-permute-start(bf16[2,3,8,16,128]{4,3,2,1,0:T(8,128)(2,1)S(1)} %pad_maximum_fusion.3.pair), channel_id=1, source_target_pairs={{0,1},{32,35},{1,2},{33,32},{2,3},{34,33},{3,0},{35,34},{4,5},{36,... | collective-permute-start | bytes 589832 | tf_op jit(solution)/shard_map/ppermute | solution.py:415
  145.7 17.9 %all-to-all-start.3 = ((f32[8,8,256]{2,1,0:T(8,128)}), f32[8,8,256]{2,1,0:T(8,128)S(1)}, u32[]{:S(2)}, u32[]{:S(2)}) async-start(f32[8,8,256]{2,1,0:T(8,128)} %get-tuple-element.32), calls=%async_computation.3 | async-start | bytes 131072 | tf_op jit(solution)/shard_map/all_to_all | solution.py:531
  152.7 10.9 %copy-start.15 = (f32[256]{0:T(256)S(1)}, f32[256]{0:T(256)}, u32[]{:S(2)}) copy-start(f32[256]{0:T(256)} %param.14) | copy-start | bytes 3076
  152.7 10.9 %copy-start.16 = (f32[256]{0:T(256)S(1)}, f32[256]{0:T(256)}, u32[]{:S(2)}) copy-start(f32[256]{0:T(256)} %param.15) | copy-start | bytes 3076
  154.2 9.4 %copy-start.1 = (bf16[3,2,8,2,2,16,256]{6,5,4,3,2,1,0:T(8,128)(2,1)S(1)}, bf16[3,2,8,2,2,16,256]{6,5,4,3,2,1,0:T(8,128)(2,1)}, u32[]{:S(2)}) copy-start(bf16[3,2,8,2,2,16,256]{6,5,4,3,2,1,0:T(8,128)(2,1)} %get-tuple-element.31) | copy-start | bytes 4718596
  167.3 10.6 %all-to-all-start.5 = ((f32[4,8,256]{2,1,0:T(8,128)}), f32[4,8,256]{2,1,0:T(8,128)S(1)}, u32[]{:S(2)}, u32[]{:S(2)}) async-start(f32[4,8,256]{2,1,0:T(8,128)} %get-tuple-element.38), calls=%async_computation.5 | async-start | bytes 65536 | tf_op jit(solution)/shard_map/all_to_all | solution.py:536
  179.6 25.6 %all-to-all-start.6 = ((bf16[8,80,256]{2,1,0:T(8,128)(2,1)}), bf16[8,80,256]{2,1,0:T(8,128)(2,1)S(1)}, u32[]{:S(2)}, u32[]{:S(2)}) async-start(bf16[8,80,256]{2,1,0:T(8,128)(2,1)} %shard_map.137), calls=%async_computation.6 | async-start | bytes 655360 | tf_op jit(solution)/shard_map/all_to_all | solution.py:545
  188.5 16.7 %copy-start.8 = (f32[512,256]{1,0:T(8,128)S(1)}, f32[512,256]{1,0:T(8,128)}, u32[]{:S(2)}) copy-start(f32[512,256]{1,0:T(8,128)} %copy-done.7) | copy-start | bytes 1572868
  (9 other events, 9.0 us)
Sparse Core Ops, SparseCore 0:
  58.8 63.6 all-gather.2

commit v3 on v2

--- a/solution.py
+++ b/solution.py
@@ -22,9 +22,12 @@
     return 0.5 * jnp.tanh(0.5 * v) + 0.5
 
 
-def transpose_kernel(cot_ref, out_ref):
-    for k in range(4):
-        out_ref[k] = cot_ref[k, 0:4].reshape(512, 256).astype(F32).T.astype(BF)
+def transpose_kernel(meta, pair, rest, out_ref):
+    core, h = meta[0], meta[2]
+    side = 2 * core - 1
+    for k, slot in enumerate((pair.at[0], pair.at[1], rest.at[0], rest.at[1])):
+        j = (h + 2 * k if k < 2 else h + side * (2 * k - 3)) & 3
+        out_ref[j] = slot[0:4].reshape(512, 256).astype(F32).T.astype(BF)
 
 
 def group_matrix(channels, per_group):
@@ -162,24 +165,20 @@
                 window = act[dc, lag : lag + 3, dr : dr + 8].reshape(384, 512)
                 term = dot(window, w[tap * 512 : tap * 512 + 512, :])
                 total = term if total is None else total + term
-    out_ref[...] = (acc + total).astype(BF).reshape(3, 8, 16, 128)
-
-
-def upsample_kernel(meta, pair, rest, mine, other, up_ref, sums_ref, w, sem):
-    core, h = meta[0], meta[2]
-    copies = []
-    for j in range(4):
-        hop, two = (h - j) & 1, ((h - j) >> 1) & 1
-        slot = jnp.where(hop == 0, two, jnp.where(core == 0, 2 + two, 3 - two))
-        at = slot * 128
-        for side, source in ((core, mine), (1 - core, other)):
-            rows = pl.ds(pl.multiple_of(at + side * 64, 64), 64)
-            copies.append(pltpu.make_async_copy(source.at[j], w.at[rows], sem))
+    refined = (acc + total).astype(BF).reshape(3, 8, 16, 128)
+    for k in range(4):
+        out_ref[k] = refined
+
+
+def upsample_kernel(ref_ref, got_ref, up_ref, sums_ref, w, sem):
+    copies = [
+        pltpu.make_async_copy(got_ref.at[j], w.at[pl.ds(j * 128, 128)], sem) for j in range(4)
+    ]
     for c in copies:
         c.start()
     for c in copies:
         c.wait()
-    x = jnp.concatenate([r[k].reshape(384, 128) for r in (pair, rest) for k in range(2)], axis=1)
+    x = jnp.concatenate([ref_ref[j].reshape(384, 128) for j in range(4)], axis=1)
     first = jnp.zeros((1, 256), F32)
     second = jnp.zeros((1, 256), F32)
     for p in range(2):
@@ -195,8 +194,8 @@
     sums_ref[...] = jnp.broadcast_to(rows[None], sums_ref.shape)
 
 
-def grad_active_kernel(meta, cot_ref, got_ref, out_ref, w_ref, q, edges, sem):
-    h = meta[2]
+def grad_active_kernel(meta, pair, rest, got_ref, out_ref, w_ref, q, edges, sem):
+    own_core, h = meta[0], meta[2]
     copies = []
     for core in range(2):
         lanes = pl.ds(core * 128, 128)
@@ -225,8 +224,12 @@
     for c in copies:
         c.start()
     for row in range(6):
-        block = jnp.clip(h + (row + 3) // 4 - 1, 0, 3)
-        v = cot_ref[block, :, (row + 3) % 4]
+        if row == 0:
+            v = rest[own_core, :, 3]
+        elif row == 5:
+            v = rest[1 - own_core, :, 0]
+        else:
+            v = pair[0, :, row - 1]
         if row == 0:
             v = jnp.where(h > 0, v, jnp.zeros_like(v))
         if row == 5:
@@ -419,6 +422,10 @@
     return lax.optimization_barrier((v, *others))[0]
 
 
+def in_hbm(v):
+    return pltpu.with_memory_space_constraint(v, pltpu.HBM)
+
+
 def struct(shape, dtype):
     return jax.ShapeDtypeStruct(shape, dtype)
 
@@ -451,6 +458,8 @@
     meta = jnp.stack([core, t, h, x]).astype(jnp.int32)
     gain2, shift2 = gain_block[None], shift_block[None]
 
+    up_w = lax.all_gather(up_weight, "height")
+
     piece = lax.dynamic_slice(conv_latent, (x * 432 + core * 208, 0), (224, 128))
     half = lax.dynamic_slice(conv_block, (0, core * 128), (216, 128))
     window = jnp.where(h % 2 == 0, jnp.pad(half, ((0, 8), (0, 0))), jnp.pad(half, ((8, 0), (0, 0))))
@@ -473,60 +482,56 @@
         pair_z[1, 224:], down_z[1, 224:], plus_6, up_z[0, 224:],
     ]
     ordered = lax.dynamic_slice(jnp.stack(steps + steps), ((8 - t) % 8, 0, 0), (8, 64, 128))
-    block_w = lax.all_gather(ordered, ("x", "core", "height"))
-    block_w = block_w.reshape(4, 2, 4, 8, 64, 128)
 
     pair_x = jnp.stack([rows, ring_step(rows, "x", 4, 2)])
     lat = call(latent_pack_kernel, struct((4, 656, 128), BF), [VM] * 6)(
         latent, one_back, two_back, stats_latent, gain_latent[None], shift_latent[None]
     )
     lat_all = lax.all_to_all(lat, "height", 0, 0, tiled=True)
-    pair_x = after(pair_x, lat_all)
+    phased = cotangent.reshape(4, 4, 16, 2, 256).transpose(0, 1, 3, 2, 4)
+    phased = after(phased, stats_latent)
+    six = jnp.concatenate([phased, later(phased[:2], -1)], 0)
+    cot_pair = jnp.stack([six, ring_step(six, "height", 4, 2)])
+    pair_x = after(pair_x, lat_all, cot_pair)
     rest_x = ring_step(pair_x, "x", 4, 1)
     other_pair = swapped(pair_x)
-
-    up_piece = lax.dynamic_slice(up_weight, (core * 64, 0), (64, 2048))
-    up_w = gathered(after(up_piece, lat_all), "height", 4)
-    phased = cotangent.reshape(4, 4, 16, 2, 256).transpose(0, 1, 3, 2, 4)
-    phased = after(phased, lat_all)
-    six = jnp.concatenate([phased, later(phased[:2], -1)], 0)
-    six = after(six, up_w)
-    other_rest = swapped(after(rest_x, up_w, six))
+    block_w = lax.all_gather(after(ordered, pair_x, up_w), ("x", "core", "height"))
+    block_w = block_w.reshape(4, 2, 4, 8, 64, 128)
+
+    cot_rest = ring_step(cot_pair, "height", 4, 1)
+    other_rest = swapped(after(rest_x, cot_rest))
 
     refined = call(
         latent_conv_kernel,
-        struct((3, 8, 16, 128), BF),
+        struct((4, 3, 8, 16, 128), BF),
         [SM, VM] + [HB] * 4,
         [
             pltpu.VMEM((3, 5, 10, 16, 512), BF),
             pltpu.VMEM((13824, 128), BF),
             pltpu.SemaphoreType.DMA,
         ],
-    )(meta, lat_all, pair_x, rest_x, other_pair, other_rest)
-    pair_y = jnp.stack([refined, ring_step(refined, "height", 4, 2)])
-    rest_y = ring_step(pair_y, "height", 4, 1)
-
-    up_w_other = swapped(after(up_w, refined))
-    cot_all = gathered(six, "height", 4)
-    cot_t = call(transpose_kernel, struct((4, 256, 512), BF), [VM])(cot_all)
+    )(meta, lat_all, *[in_hbm(v) for v in (pair_x, rest_x, other_pair, other_rest)])
+    refined_all = lax.all_to_all(refined, "height", 0, 0, tiled=True)
+
+    cot_t = call(transpose_kernel, struct((4, 256, 512), BF), [SM, VM, VM])(meta, cot_pair, cot_rest)
     grad_active, weight = call(
         grad_active_kernel,
         [struct((512, 256), F32), struct((8, 864, 256), BF)],
-        [SM, VM, HB],
+        [SM, VM, VM, HB],
         [
             pltpu.VMEM((6, 6, 4, 16, 256), BF),
             pltpu.VMEM((2, 4, 8, 16, 128), BF),
             pltpu.SemaphoreType.DMA,
         ],
-    )(meta, after(cot_all, cot_t), block_w)
+    )(meta, after(cot_pair, cot_t), cot_rest, block_w)
     weight = weight.reshape(6912, 256)
 
     up, up_sums = call(
         upsample_kernel,
         [struct((3, 2, 8, 2, 2, 16, 256), BF), struct((8, 8, 256), F32)],
-        [SM, VM, VM, HB, HB],
+        [VM, HB],
         [pltpu.VMEM((512, 2048), BF), pltpu.SemaphoreType.DMA],
-    )(meta, pair_y, rest_y, up_w, up_w_other)
+    )(refined_all, up_w)
     up = up.reshape(6, 16, 2, 16, 256)
     stats_block = lax.all_to_all(up_sums, "tm", 0, 0, tiled=True)
 

time: 216 us -> 204 us (0.944)
  the two profiles are of different devices: /device:TPU:2 before, /device:TPU:8 now
where the time goes in v3:
time: 204 us; the launch traced here: 202 us
  starting transfers between devices  85.9 us (42%)
  waiting for transfers between devices  41.1 us (20%)
  Pallas kernels  32.5 us (16%)
  between operations  14.6 us (7%)
  local copies, waits for them, and re-layouts  12.5 us (6%)
  blocking collectives  12.3 us (6%)
  other arithmetic  3.24 us (2%)
    ppermute x4, waiting for transfers between devices, ring_step(): lax.ppermute(v, ('x', 'core') if axis == 'x' else ('core', axis), pairs)  17.8 us
    ppermute x4, starting transfers between devices, ring_step(): lax.ppermute(v, ('x', 'core') if axis == 'x' else ('core', axis), pairs)  14.5 us
    all_to_all x1, waiting for transfers between devices, local(): got = lax.all_to_all(packed, 'tm', 0, 0, tiled=True)  13 us
    all_to_all x1, blocking collectives, local(): refined_all = lax.all_to_all(refined, 'height', 0, 0, tiled=True)  12.3 us
    all_to_all x1, starting transfers between devices, local(): stats_block = lax.all_to_all(up_sums, 'tm', 0, 0, tiled=True)  11.8 us
    ppermute x2, starting transfers between devices, along_z_by_core(): return lax.ppermute(v, ('zh', 'core', 'tm'), pairs)  11.4 us
    all_to_all x1, starting transfers between devices, local(): got = lax.all_to_all(packed, 'tm', 0, 0, tiled=True)  10 us
    ppermute x3, starting transfers between devices, later(): lax.ppermute(v, 'tm', [(i, i + step) for i in range(8) if 0 <= i + step <...  9.93 us
  transfers between devices with their start and end apart: 20, of which 8 were waited for; matrix products, arithmetic and copies ran while one was open for 3% of the time, Pallas kernels for 14%

profile of v3, /device:TPU:8, one launch (start us, length us, event | category | flops | bytes accessed | tf_op | source)
XLA Modules:
  0.0 202.2 jit_solution(2251439456319630897)
XLA Ops:
  8.3 9.1 %collective-permute-start.2 = (bf16[288,128]{1,0:T(8,128)(2,1)S(1)}, bf16[288,128]{1,0:T(8,128)(2,1)S(1)}, u32[]{:S(2)}, u32[]{:S(2)}) collective-permute-start(bf16[288,128]{1,0:T(8,128)(2,1)S(1)} %get-tuple-element.42), channel_id=1, source_target_pairs={{0,16},{32,112},{4,20},{36,116},{8,24},{40,120},{12,28},{44,124},{... | collective-permute-start | bytes 221192 | tf_op jit(solution)/shard_map/ppermute | solution.py:406
  17.4 3.8 %collective-permute-start = (bf16[2,8,16,128]{3,2,1,0:T(8,128)(2,1)}, bf16[2,8,16,128]{3,2,1,0:T(8,128)(2,1)S(1)}, u32[]{:S(2)}, u32[]{:S(2)}) collective-permute-start(bf16[2,8,16,128]{3,2,1,0:T(8,128)(2,1)} %x_ref.3), channel_id=1, source_target_pairs={{0,4},{4,8},{8,12},{12,16},{16,20},{20,24},{24,28},{1,5},{5,9},{9,... | collective-permute-start | bytes 196616 | tf_op jit(solution)/shard_map/ppermute | solution.py:393
  22.7 8.5 %all-to-all-start = ((f32[8,8,128]{2,1,0:T(8,128)}), f32[8,8,128]{2,1,0:T(8,128)S(1)}, u32[]{:S(2)}, u32[]{:S(2)}) async-start(f32[8,8,128]{2,1,0:T(8,128)} %shard_map.128), calls=%async_computation | async-start | bytes 65536 | tf_op jit(solution)/shard_map/all_to_all | solution.py:470
  32.0 4.8 %collective-permute-start.1 = (bf16[1,8,16,128]{3,2,1,0:T(8,128)(2,1)S(1)}, bf16[1,8,16,128]{3,2,1,0:T(8,128)(2,1)S(1)}, u32[]{:S(2)}, u32[]{:S(2)}) collective-permute-start(bf16[1,8,16,128]{3,2,1,0:T(8,128)(2,1)S(1)} %slice.48), channel_id=1, source_target_pairs={{0,8},{4,12},{8,16},{12,20},{16,24},{20,28},{1,9},{5,13},{9,17},{1... | collective-permute-start | bytes 98312 | tf_op jit(solution)/shard_map/ppermute | solution.py:393
  38.4 3.5 %all-to-all-done.stats_ref = f32[8,8,128]{2,1,0:T(8,128)S(1)} async-done(((f32[8,8,128]{2,1,0:T(8,128)}), f32[8,8,128]{2,1,0:T(8,128)S(1)}, u32[]{:S(2)}, u32[]{:S(2)}) %all-to-all-start) | async-done | bytes 32800 | tf_op jit(solution)/shard_map/all_to_all | solution.py:470
  41.8 2.3 %collective-permute-start.5 = (bf16[2,288,128]{2,1,0:T(8,128)(2,1)S(1)}, bf16[2,288,128]{2,1,0:T(8,128)(2,1)S(1)}, u32[]{:S(2)}, u32[]{:S(2)}) collective-permute-start(bf16[2,288,128]{2,1,0:T(8,128)(2,1)S(1)} %pad_maximum_fusion.3), channel_id=1, source_target_pairs={{0,8},{32,120},{4,12},{36,124},{8,16},{40,32},{12,20},{44,36},{16,... | collective-permute-start | bytes 442376 | tf_op jit(solution)/shard_map/ppermute | solution.py:406
  44.1 4.7 %collective-permute-start.4 = (bf16[2,288,128]{2,1,0:T(8,128)(2,1)S(1)}, bf16[2,288,128]{2,1,0:T(8,128)(2,1)S(1)}, u32[]{:S(2)}, u32[]{:S(2)}) collective-permute-start(bf16[2,288,128]{2,1,0:T(8,128)(2,1)S(1)} %pad_maximum_fusion.3), channel_id=1, source_target_pairs={{0,92},{4,0},{8,4},{12,8},{16,12},{20,16},{24,20},{28,24},{64,28},... | collective-permute-start | bytes 442376 | tf_op jit(solution)/shard_map/ppermute | solution.py:397
  48.8 1.9 collective-permute-start.3
  50.8 1.3 collective-permute-start.7
  53.1 4.9 %all-to-all-start.1 = ((bf16[4,656,128]{2,1,0:T(8,128)(2,1)}), bf16[4,656,128]{2,1,0:T(8,128)(2,1)S(1)}, u32[]{:S(2)}, u32[]{:S(2)}) async-start(bf16[4,656,128]{2,1,0:T(8,128)(2,1)} %shard_map.129), calls=%async_computation.1 | async-start | bytes 1343488 | tf_op jit(solution)/shard_map/all_to_all | solution.py:490
  58.0 4.0 %collective-permute-start.8 = (bf16[6,4,2,16,256]{4,3,2,1,0:T(8,128)(2,1)S(1)}, bf16[6,4,2,16,256]{4,3,2,1,0:T(8,128)(2,1)}, u32[]{:S(2)}, u32[]{:S(2)}) collective-permute-start(bf16[6,4,2,16,256]{4,3,2,1,0:T(8,128)(2,1)S(1)} %constant_dynamic-update-slice_fusion), channel_id=1, source_target_pairs={{0,2},{32,34},{1,3},{33,35},{2,0},{34,32},{3,1},{35,33},{4,6},{36,... | collective-permute-start | bytes 1179656 | tf_op jit(solution)/shard_map/ppermute | solution.py:418
  63.0 4.9 %collective-permute-start.6 = (bf16[8,224,128]{2,1,0:T(8,128)(2,1)}, bf16[8,224,128]{2,1,0:T(8,128)(2,1)}, u32[]{:S(2)}, u32[]{:S(2)}) collective-permute-start(bf16[8,224,128]{2,1,0:T(8,128)(2,1)} %get-tuple-element.40), channel_id=1, source_target_pairs={{0,256},{32,288},{128,384},{160,416},{256,0},{288,32},{384,128},{4... | collective-permute-start | bytes 1376264 | tf_op jit(solution)/shard_map/ppermute | solution.py:418
  68.8 6.9 %collective-permute-done.8 = bf16[6,4,2,16,256]{4,3,2,1,0:T(8,128)(2,1)} collective-permute-done((bf16[6,4,2,16,256]{4,3,2,1,0:T(8,128)(2,1)S(1)}, bf16[6,4,2,16,256]{4,3,2,1,0:T(8,128)(2,1)}, u32[]{:S(2)}, u32[]{:S(2)}) %collective-permute-start.8) | collective-permute-done | bytes 393248 | tf_op jit(solution)/shard_map/ppermute | solution.py:418
  78.8 3.7 %collective-permute-start.9 = (bf16[2,8,224,128]{3,2,1,0:T(8,128)(2,1)S(1)}, bf16[2,8,224,128]{3,2,1,0:T(8,128)(2,1)S(1)}, u32[]{:S(2)}, u32[]{:S(2)}) collective-permute-start(bf16[2,8,224,128]{3,2,1,0:T(8,128)(2,1)S(1)} %pad_maximum_fusion.m0), channel_id=1, source_target_pairs={{0,128},{32,416},{128,256},{160,32},{256,384},{288,160},{384,0},{4... | collective-permute-start | bytes 2752520 | tf_op jit(solution)/shard_map/ppermute | solution.py:418
  82.5 1.9 collective-permute-start.11
  84.4 1.9 collective-permute-start.10
  86.3 10.0 %collective-permute-done.11.rest = bf16[2,6,4,2,16,256]{5,4,3,2,1,0:T(8,128)(2,1)S(1)} collective-permute-done((bf16[2,6,4,2,16,256]{5,4,3,2,1,0:T(8,128)(2,1)S(1)}, bf16[2,6,4,2,16,256]{5,4,3,2,1,0:T(8,128)(2,1)S(1)}, u32[]{:S(2)}, u32[]{:S(2)}) %collective-permute-start.11) | collective-permute-done | bytes 786464 | tf_op jit(solution)/shard_map/ppermute | solution.py:418
  96.4 1.9 collective-permute-start.12
  98.4 2.4 %collective-permute-done.12.o1 = bf16[2,8,224,128]{3,2,1,0:T(8,128)(2,1)S(1)} collective-permute-done((bf16[2,8,224,128]{3,2,1,0:T(8,128)(2,1)S(1)}, bf16[2,8,224,128]{3,2,1,0:T(8,128)(2,1)S(1)}, u32[]{:S(2)}, u32[]{:S(2)}) %collective-permute-start.12) | collective-permute-done | bytes 917536 | tf_op jit(solution)/shard_map/ppermute | solution.py:389
  101.7 5.5 %shard_map.130 = bf16[4,3,8,16,128]{4,3,2,1,0:T(8,128)(2,1)S(1)} custom-call(s32[4]{0:T(128)S(1)} %pad_add_fusion.meta, bf16[4,656,128]{2,1,0:T(8,128)(2,1)S(1)} %all-to-all-done.1.lat_ref, bf16[2,8,224,128]{3,2,1,0:T(8,128)(2,1)} %copy-done.16, bf16[2,8,224,128]{3,2,1,0:T(8,128)(2,1)} %copy-done.17, bf16[2,8,224,128]{3,2,1,0:T(8,128)(2,1)} %copy-done.18, ...), custom_call_target="tpu_custom_call" | custom-call | tf_op jit(solution)/shard_map/pallas_call | solution.py:504
  107.2 12.3 %all_to_all.30.ref_ref = bf16[4,3,8,16,128]{4,3,2,1,0:T(8,128)(2,1)S(1)} all-to-all(bf16[4,3,8,16,128]{4,3,2,1,0:T(8,128)(2,1)S(1)} %shard_map.130), channel_id=1, replica_groups=mesh['x'=4,'zh'=2,'core'=2,'tm'=8,'height'=4] {'height'}, dimensions={0} | all-to-all | bytes 786432 | tf_op jit(solution)/shard_map/all_to_all | solution.py:514
  119.5 1.8 shard_map.131
  121.3 11.8 %all-to-all-start.3 = ((f32[8,8,256]{2,1,0:T(8,128)}), f32[8,8,256]{2,1,0:T(8,128)S(1)}, u32[]{:S(2)}, u32[]{:S(2)}) async-start(f32[8,8,256]{2,1,0:T(8,128)} %get-tuple-element.27), calls=%async_computation.3 | async-start | bytes 131072 | tf_op jit(solution)/shard_map/all_to_all | solution.py:536
  136.2 4.1 %all-gather.7.cloned.1.call-done = bf16[256,64,128]{2,1,0:T(8,128)(2,1)} async-done(((bf16[8,64,128]{2,1,0:T(8,128)(2,1)}), bf16[256,64,128]{2,1,0:T(8,128)(2,1)}) %all-gather.7.cloned.1.call-update) | async-done | bytes 4194320 | tf_op jit(solution)/shard_map/all_gather | solution.py:498
  141.4 6.0 %shard_map.134 = (f32[512,256]{1,0:T(8,128)S(1)}, bf16[8,864,256]{2,1,0:T(8,128)(2,1)}) custom-call(s32[4]{0:T(128)S(1)} %pad_add_fusion.meta, bf16[2,6,4,2,16,256]{5,4,3,2,1,0:T(8,128)(2,1)S(1)} %pad_maximum_fusion.1.pair, bf16[2,6,4,2,16,256]{5,4,3,2,1,0:T(8,128)(2,1)S(1)} %copy-done.5, bf16[4,2,4,8,64,128]{5,4,3,2,1,0:T(8,128)(2,1)} %bitcast.38), custom_call_target="tpu_custom_call" | custom-call | tf_op jit(solution)/shard_map/pallas_call | solution.py:517
  149.3 1.9 shard_map.136
  151.1 4.5 %all-to-all-start.4 = ((f32[4,8,256]{2,1,0:T(8,128)}), f32[4,8,256]{2,1,0:T(8,128)S(1)}, u32[]{:S(2)}, u32[]{:S(2)}) async-start(f32[4,8,256]{2,1,0:T(8,128)} %get-tuple-element.34), calls=%async_computation.4 | async-start | bytes 65536 | tf_op jit(solution)/shard_map/all_to_all | solution.py:541
  156.9 6.4 %shard_map.133 = (bf16[8,72,256]{2,1,0:T(8,128)(2,1)S(1)}, bf16[6,18,4,16,256]{4,3,2,1,0:T(8,128)(2,1)}) custom-call(s32[4]{0:T(128)S(1)} %pad_add_fusion.meta, bf16[6,16,2,16,256]{4,3,2,1,0:T(8,128)(2,1)S(1)} %bitcast.27, f32[8,8,256]{2,1,0:T(8,128)S(1)} %all-to-all-done.3.stats_ref, f32[1,256]{1,0:T(1,128)S(1)} %bitcast.32, f32[1,256]{1,0:T(1,128)S(1)} %bitcast.35, ...), custom_call_target="tpu_custom_call" | custom-call | tf_op jit(solution)/shard_map/pallas_call | solution.py:543
  164.0 10.0 %all-to-all-start.5 = ((bf16[8,80,256]{2,1,0:T(8,128)(2,1)}), bf16[8,80,256]{2,1,0:T(8,128)(2,1)S(1)}, u32[]{:S(2)}, u32[]{:S(2)}) async-start(bf16[8,80,256]{2,1,0:T(8,128)(2,1)} %shard_map.137), calls=%async_computation.5 | async-start | bytes 655360 | tf_op jit(solution)/shard_map/all_to_all | solution.py:550
  174.0 5.8 %shard_map.135 = bf16[4,4,32,256]{3,2,1,0:T(8,128)(2,1)} custom-call(s32[4]{0:T(128)S(1)} %pad_add_fusion.meta, bf16[6,16,2,16,256]{4,3,2,1,0:T(8,128)(2,1)S(1)} %bitcast.28, bf16[6,18,4,16,256]{4,3,2,1,0:T(8,128)(2,1)} %get-tuple-element.28.q_ref, bf16[6912,256]{1,0:T(8,128)(2,1)} %bitcast.39), custom_call_target="tpu_custom_call" | custom-call | tf_op jit(solution)/shard_map/pallas_call | solution.py:552
  179.9 13.0 %all-to-all-done.5.got_ref = bf16[8,80,256]{2,1,0:T(8,128)(2,1)S(1)} async-done(((bf16[8,80,256]{2,1,0:T(8,128)(2,1)}), bf16[8,80,256]{2,1,0:T(8,128)(2,1)S(1)}, u32[]{:S(2)}, u32[]{:S(2)}) %all-to-all-start.5) | async-done | bytes 327712 | tf_op jit(solution)/shard_map/all_to_all | solution.py:550
  192.9 1.9 shard_map.138
  (99 shorter events, 20.3 us)
Async XLA Ops:
  7.2 44.9 %copy-start.11 = (bf16[2,8,16,128]{3,2,1,0:T(8,128)(2,1)S(1)}, bf16[2,8,16,128]{3,2,1,0:T(8,128)(2,1)}, u32[]{:S(2)}) copy-start(bf16[2,8,16,128]{3,2,1,0:T(8,128)(2,1)} %x_ref.3) | copy-start | bytes 196612
  7.2 44.9 %copy-start.15 = (f32[128]{0:T(128)S(1)}, f32[128]{0:T(128)}, u32[]{:S(2)}) copy-start(f32[128]{0:T(128)} %param.11) | copy-start | bytes 1540
  7.2 44.9 %copy-start.14 = (f32[128]{0:T(128)S(1)}, f32[128]{0:T(128)}, u32[]{:S(2)}) copy-start(f32[128]{0:T(128)} %param.10) | copy-start | bytes 1540
  7.2 71.5 %all-gather.5.cloned.1.call-start = ((), (), s32[]{:S(2)}) async-start(), calls=%async_computation.6 | async-start | bytes 2621440 | tf_op jit(solution)/shard_map/all_gather | solution.py:461
  8.3 29.8 %collective-permute-start.2 = (bf16[288,128]{1,0:T(8,128)(2,1)S(1)}, bf16[288,128]{1,0:T(8,128)(2,1)S(1)}, u32[]{:S(2)}, u32[]{:S(2)}) collective-permute-start(bf16[288,128]{1,0:T(8,128)(2,1)S(1)} %get-tuple-element.42), channel_id=1, source_target_pairs={{0,16},{32,112},{4,20},{36,116},{8,24},{40,120},{12,28},{44,124},{... | collective-permute-start | bytes 221192 | tf_op jit(solution)/shard_map/ppermute | solution.py:406
  17.4 21.0 %collective-permute-start = (bf16[2,8,16,128]{3,2,1,0:T(8,128)(2,1)}, bf16[2,8,16,128]{3,2,1,0:T(8,128)(2,1)S(1)}, u32[]{:S(2)}, u32[]{:S(2)}) collective-permute-start(bf16[2,8,16,128]{3,2,1,0:T(8,128)(2,1)} %x_ref.3), channel_id=1, source_target_pairs={{0,4},{4,8},{8,12},{12,16},{16,20},{20,24},{24,28},{1,5},{5,9},{9,... | collective-permute-start | bytes 196616 | tf_op jit(solution)/shard_map/ppermute | solution.py:393
  22.7 19.1 %all-to-all-start = ((f32[8,8,128]{2,1,0:T(8,128)}), f32[8,8,128]{2,1,0:T(8,128)S(1)}, u32[]{:S(2)}, u32[]{:S(2)}) async-start(f32[8,8,128]{2,1,0:T(8,128)} %shard_map.128), calls=%async_computation | async-start | bytes 65536 | tf_op jit(solution)/shard_map/all_to_all | solution.py:470
  32.0 6.4 %collective-permute-start.1 = (bf16[1,8,16,128]{3,2,1,0:T(8,128)(2,1)S(1)}, bf16[1,8,16,128]{3,2,1,0:T(8,128)(2,1)S(1)}, u32[]{:S(2)}, u32[]{:S(2)}) collective-permute-start(bf16[1,8,16,128]{3,2,1,0:T(8,128)(2,1)S(1)} %slice.48), channel_id=1, source_target_pairs={{0,8},{4,12},{8,16},{12,20},{16,24},{20,28},{1,9},{5,13},{9,17},{1... | collective-permute-start | bytes 98312 | tf_op jit(solution)/shard_map/ppermute | solution.py:393
  41.8 20.2 %collective-permute-start.5 = (bf16[2,288,128]{2,1,0:T(8,128)(2,1)S(1)}, bf16[2,288,128]{2,1,0:T(8,128)(2,1)S(1)}, u32[]{:S(2)}, u32[]{:S(2)}) collective-permute-start(bf16[2,288,128]{2,1,0:T(8,128)(2,1)S(1)} %pad_maximum_fusion.3), channel_id=1, source_target_pairs={{0,8},{32,120},{4,12},{36,124},{8,16},{40,32},{12,20},{44,36},{16,... | collective-permute-start | bytes 442376 | tf_op jit(solution)/shard_map/ppermute | solution.py:406
  44.1 17.9 %collective-permute-start.4 = (bf16[2,288,128]{2,1,0:T(8,128)(2,1)S(1)}, bf16[2,288,128]{2,1,0:T(8,128)(2,1)S(1)}, u32[]{:S(2)}, u32[]{:S(2)}) collective-permute-start(bf16[2,288,128]{2,1,0:T(8,128)(2,1)S(1)} %pad_maximum_fusion.3), channel_id=1, source_target_pairs={{0,92},{4,0},{8,4},{12,8},{16,12},{20,16},{24,20},{28,24},{64,28},... | collective-permute-start | bytes 442376 | tf_op jit(solution)/shard_map/ppermute | solution.py:397
  48.8 13.3 %collective-permute-start.3 = (bf16[2,288,128]{2,1,0:T(8,128)(2,1)S(1)}, bf16[2,288,128]{2,1,0:T(8,128)(2,1)S(1)}, u32[]{:S(2)}, u32[]{:S(2)}) collective-permute-start(bf16[2,288,128]{2,1,0:T(8,128)(2,1)S(1)} %pad_maximum_fusion.3), channel_id=1, source_target_pairs={{0,4},{4,8},{8,12},{12,16},{16,20},{20,24},{24,28},{28,64},{64,68}... | collective-permute-start | bytes 442376 | tf_op jit(solution)/shard_map/ppermute | solution.py:397
  50.8 7.3 %collective-permute-start.7 = (bf16[2,4,2,16,256]{4,3,2,1,0:T(8,128)(2,1)S(1)}, bf16[2,4,2,16,256]{4,3,2,1,0:T(8,128)(2,1)S(1)}, u32[]{:S(2)}, u32[]{:S(2)}) collective-permute-start(bf16[2,4,2,16,256]{4,3,2,1,0:T(8,128)(2,1)S(1)} %slice.53), channel_id=1, source_target_pairs={{4,0},{8,4},{12,8},{16,12},{20,16},{24,20},{28,24},{5,1},{9,5},{13... | collective-permute-start | bytes 393224 | tf_op jit(solution)/shard_map/ppermute | solution.py:393
  53.1 25.6 %all-to-all-start.1 = ((bf16[4,656,128]{2,1,0:T(8,128)(2,1)}), bf16[4,656,128]{2,1,0:T(8,128)(2,1)S(1)}, u32[]{:S(2)}, u32[]{:S(2)}) async-start(bf16[4,656,128]{2,1,0:T(8,128)(2,1)} %shard_map.129), calls=%async_computation.1 | async-start | bytes 1343488 | tf_op jit(solution)/shard_map/all_to_all | solution.py:490
  58.0 82.2 %all-gather.7.cloned.1.call-start = ((), (), s32[]{:S(2)}) async-start(), calls=%async_computation.7 | async-start | bytes 4325376 | tf_op jit(solution)/shard_map/all_gather | solution.py:498
  58.0 17.6 %collective-permute-start.8 = (bf16[6,4,2,16,256]{4,3,2,1,0:T(8,128)(2,1)S(1)}, bf16[6,4,2,16,256]{4,3,2,1,0:T(8,128)(2,1)}, u32[]{:S(2)}, u32[]{:S(2)}) collective-permute-start(bf16[6,4,2,16,256]{4,3,2,1,0:T(8,128)(2,1)S(1)} %constant_dynamic-update-slice_fusion), channel_id=1, source_target_pairs={{0,2},{32,34},{1,3},{33,35},{2,0},{34,32},{3,1},{35,33},{4,6},{36,... | collective-permute-start | bytes 1179656 | tf_op jit(solution)/shard_map/ppermute | solution.py:418
  63.0 14.6 %collective-permute-start.6 = (bf16[8,224,128]{2,1,0:T(8,128)(2,1)}, bf16[8,224,128]{2,1,0:T(8,128)(2,1)}, u32[]{:S(2)}, u32[]{:S(2)}) collective-permute-start(bf16[8,224,128]{2,1,0:T(8,128)(2,1)} %get-tuple-element.40), channel_id=1, source_target_pairs={{0,256},{32,288},{128,384},{160,416},{256,0},{288,32},{384,128},{4... | collective-permute-start | bytes 1376264 | tf_op jit(solution)/shard_map/ppermute | solution.py:418
  78.7 22.0 %copy-start.16 = (bf16[2,8,224,128]{3,2,1,0:T(8,128)(2,1)}, bf16[2,8,224,128]{3,2,1,0:T(8,128)(2,1)S(1)}, u32[]{:S(2)}) copy-start(bf16[2,8,224,128]{3,2,1,0:T(8,128)(2,1)S(1)} %pad_maximum_fusion.m0) | copy-start | bytes 2752516
  78.8 40.7 %copy-start.6 = (bf16[512,2048]{1,0:T(8,128)(2,1)S(1)}, bf16[512,2048]{1,0:T(8,128)(2,1)}, u32[]{:S(2)}) copy-start(bf16[512,2048]{1,0:T(8,128)(2,1)} %all-gather.5.cloned.1.call-done) | copy-start | bytes 6291460
  78.8 17.6 %collective-permute-start.9 = (bf16[2,8,224,128]{3,2,1,0:T(8,128)(2,1)S(1)}, bf16[2,8,224,128]{3,2,1,0:T(8,128)(2,1)S(1)}, u32[]{:S(2)}, u32[]{:S(2)}) collective-permute-start(bf16[2,8,224,128]{3,2,1,0:T(8,128)(2,1)S(1)} %pad_maximum_fusion.m0), channel_id=1, source_target_pairs={{0,128},{32,416},{128,256},{160,32},{256,384},{288,160},{384,0},{4... | collective-permute-start | bytes 2752520 | tf_op jit(solution)/shard_map/ppermute | solution.py:418
  82.5 13.9 %collective-permute-start.11 = (bf16[2,6,4,2,16,256]{5,4,3,2,1,0:T(8,128)(2,1)S(1)}, bf16[2,6,4,2,16,256]{5,4,3,2,1,0:T(8,128)(2,1)S(1)}, u32[]{:S(2)}, u32[]{:S(2)}) collective-permute-start(bf16[2,6,4,2,16,256]{5,4,3,2,1,0:T(8,128)(2,1)S(1)} %pad_maximum_fusion.1.pair), channel_id=1, source_target_pairs={{0,1},{32,35},{1,2},{33,32},{2,3},{34,33},{3,0},{35,34},{4,5},{36,... | collective-permute-start | bytes 2359304 | tf_op jit(solution)/shard_map/ppermute | solution.py:418
  84.4 14.0 %collective-permute-start.10 = (bf16[2,8,224,128]{3,2,1,0:T(8,128)(2,1)S(1)}, bf16[2,8,224,128]{3,2,1,0:T(8,128)(2,1)S(1)}, u32[]{:S(2)}, u32[]{:S(2)}) collective-permute-start(bf16[2,8,224,128]{3,2,1,0:T(8,128)(2,1)S(1)} %pad_maximum_fusion.m0), channel_id=1, source_target_pairs={{0,32},{32,0},{1,33},{33,1},{2,34},{34,2},{3,35},{35,3},{4,36},{36... | collective-permute-start | bytes 2752520 | tf_op jit(solution)/shard_map/ppermute | solution.py:389
  96.3 10.8 %copy-start.3 = (bf16[2,6,4,2,16,256]{5,4,3,2,1,0:T(8,128)(2,1)}, bf16[2,6,4,2,16,256]{5,4,3,2,1,0:T(8,128)(2,1)S(1)}, u32[]{:S(2)}) copy-start(bf16[2,6,4,2,16,256]{5,4,3,2,1,0:T(8,128)(2,1)S(1)} %collective-permute-done.11.rest) | copy-start | bytes 2359300
  96.4 4.4 %copy-start.17 = (bf16[2,8,224,128]{3,2,1,0:T(8,128)(2,1)}, bf16[2,8,224,128]{3,2,1,0:T(8,128)(2,1)S(1)}, u32[]{:S(2)}) copy-start(bf16[2,8,224,128]{3,2,1,0:T(8,128)(2,1)S(1)} %collective-permute-done.9.m1) | copy-start | bytes 2752516
  96.4 4.4 %collective-permute-start.12 = (bf16[2,8,224,128]{3,2,1,0:T(8,128)(2,1)S(1)}, bf16[2,8,224,128]{3,2,1,0:T(8,128)(2,1)S(1)}, u32[]{:S(2)}, u32[]{:S(2)}) collective-permute-start(bf16[2,8,224,128]{3,2,1,0:T(8,128)(2,1)S(1)} %collective-permute-done.9.m1), channel_id=1, source_target_pairs={{0,32},{32,0},{1,33},{33,1},{2,34},{34,2},{3,35},{35,3},{4,36},{36... | collective-permute-start | bytes 2752520 | tf_op jit(solution)/shard_map/ppermute | solution.py:389
  98.4 2.4 %copy-start.18 = (bf16[2,8,224,128]{3,2,1,0:T(8,128)(2,1)}, bf16[2,8,224,128]{3,2,1,0:T(8,128)(2,1)S(1)}, u32[]{:S(2)}) copy-start(bf16[2,8,224,128]{3,2,1,0:T(8,128)(2,1)S(1)} %collective-permute-done.10.o0) | copy-start | bytes 2752516
  121.3 26.9 %all-to-all-start.3 = ((f32[8,8,256]{2,1,0:T(8,128)}), f32[8,8,256]{2,1,0:T(8,128)S(1)}, u32[]{:S(2)}, u32[]{:S(2)}) async-start(f32[8,8,256]{2,1,0:T(8,128)} %get-tuple-element.27), calls=%async_computation.3 | async-start | bytes 131072 | tf_op jit(solution)/shard_map/all_to_all | solution.py:536
  134.2 14.0 %copy-start.13 = (f32[256]{0:T(256)S(1)}, f32[256]{0:T(256)}, u32[]{:S(2)}) copy-start(f32[256]{0:T(256)} %param.15) | copy-start | bytes 3076
  136.2 12.0 %copy-start.12 = (f32[256]{0:T(256)S(1)}, f32[256]{0:T(256)}, u32[]{:S(2)}) copy-start(f32[256]{0:T(256)} %param.14) | copy-start | bytes 3076
  151.1 12.1 %all-to-all-start.4 = ((f32[4,8,256]{2,1,0:T(8,128)}), f32[4,8,256]{2,1,0:T(8,128)S(1)}, u32[]{:S(2)}, u32[]{:S(2)}) async-start(f32[4,8,256]{2,1,0:T(8,128)} %get-tuple-element.34), calls=%async_computation.4 | async-start | bytes 65536 | tf_op jit(solution)/shard_map/all_to_all | solution.py:541
  155.6 1.2 copy-start.2
  164.0 28.9 %all-to-all-start.5 = ((bf16[8,80,256]{2,1,0:T(8,128)(2,1)}), bf16[8,80,256]{2,1,0:T(8,128)(2,1)S(1)}, u32[]{:S(2)}, u32[]{:S(2)}) async-start(bf16[8,80,256]{2,1,0:T(8,128)(2,1)} %shard_map.137), calls=%async_computation.5 | async-start | bytes 655360 | tf_op jit(solution)/shard_map/all_to_all | solution.py:550
  174.0 18.9 %copy-start.7 = (bf16[4,4,32,256]{3,2,1,0:T(8,128)(2,1)S(1)}, bf16[4,4,32,256]{3,2,1,0:T(8,128)(2,1)}, u32[]{:S(2)}) copy-start(bf16[4,4,32,256]{3,2,1,0:T(8,128)(2,1)} %cot_ref.1) | copy-start | bytes 786436
  (8 other events, 8.0 us)
Sparse Core Ops, SparseCore 0:
  17.5 37.1 all-gather.4
  78.9 61.3 all-gather.6
